TPU v7x, 512 devices: a whole 4x8x8 slice. The times are simulated.
512 devices in a mesh: grp: 16 (over y_hi, x, core), seq: 32 (over z, y_lo).
Axes of the slice: x: 4, y: 8 (y_hi: 2, y_lo: 4; y = y_hi * 4 + y_lo), z: 8, core: 2. Of those that a mesh axis runs over, the one named last changes fastest.
Arguments:
- query_vectors: bfloat16 [65536, 1024], P(('grp', 'seq')), may hold values from -140 to 140
- key_vectors: bfloat16 [65536, 1024], P(('grp', 'seq')), may hold values from -5 to 5
- value_vectors: bfloat16 [65536, 1024], P(('grp', 'seq')), may hold values from -6 to 6
- out_grads: bfloat16 [65536, 1024], P(('grp', 'seq')), may hold values from -6 to 6
- offsets: int32 [3, 4], replicated, may hold values from 0 to 127, as said below
Outputs:
- attended: bfloat16 [65536, 1024], P(('grp', 'seq'))
- query_grads: bfloat16 [65536, 1024], P(('grp', 'seq'))
- key_grads: bfloat16 [65536, 1024], P(('grp', 'seq'))
- value_grads: bfloat16 [65536, 1024], P(('grp', 'seq'))
Inputs may be any that keep to these rules, and one draw needn't show every extreme that they name: offsets[l, g] lies below the span of far level l + 1, that is 4, 32, 128 for l = 0, 1, 2; some head group has offset 0 at the first far level, and some head group has offset 128 - 1 at the third.
All inputs are finite; a program needn't handle non-finite values.
Results may differ from a plain program's by a relative error of at most 0.011.
Values may be sent and summed in bfloat16 or wider, within the bound.
A program may use at most 64 MiB of HBM per device.

v0:
```python
import math

import jax
import jax.numpy as jnp
from jax import lax
from jax.sharding import PartitionSpec as P

HEAD_DIM = 128
HGROUPS = 4
SPAN_A = 4


def partner_2(block, axis, apart):
    count = lax.axis_size(axis)
    route = []
    for low in range(count):
        high = low | 1 << apart
        if high != low and high < count:
            route += [(low, high), (high, low)]
    return lax.ppermute(block, axis, route)


def product(form, left, right):
    return jnp.einsum(form, left, right, preferred_element_type=jnp.float32)


def select_tiles(source, offset_row, span_size):
    row_total, feature_count = source.shape
    grouped = source.reshape(row_total // span_size, span_size, HGROUPS, feature_count // HGROUPS)
    selector = (jnp.arange(span_size, dtype=jnp.int32)[:, None] == offset_row[None, :]).astype(
        source.dtype
    )
    picked = jnp.sum(grouped * selector[None, :, :, None], axis=1)
    return picked.reshape(row_total // span_size, feature_count)


def spread_rows(tile_sums, offset_row, span_size):
    tile_rows, feature_count = tile_sums.shape
    selector = (jnp.arange(span_size, dtype=jnp.int32)[:, None] == offset_row[None, :]).astype(
        tile_sums.dtype
    )
    grouped = (
        tile_sums.reshape(tile_rows, 1, HGROUPS, feature_count // HGROUPS)
        * selector[None, :, :, None]
    )
    return grouped.reshape(tile_rows * span_size, feature_count)


def attend(queries, grads, key_rows, value_rows):
    row_count, feature_count = queries.shape
    level_count = key_rows.shape[0] // row_count
    group_width = feature_count // HGROUPS
    head_count = group_width // HEAD_DIM
    score_scale = 1.0 / math.sqrt(HEAD_DIM)
    results = ([], [], [], [])
    for group_id in range(HGROUPS):
        start_col = group_id * group_width
        query_heads = queries[:, start_col : start_col + group_width].reshape(
            row_count, head_count, HEAD_DIM
        )
        grad_heads = grads[:, start_col : start_col + group_width].reshape(
            row_count, head_count, HEAD_DIM
        )
        key_heads = key_rows[:, start_col : start_col + group_width].reshape(
            level_count * row_count, head_count, HEAD_DIM
        )
        value_heads = value_rows[:, start_col : start_col + group_width].reshape(
            level_count * row_count, head_count, HEAD_DIM
        )
        scores = product("ihd,jhd->hij", query_heads, key_heads) * score_scale
        topmost = jnp.max(scores, axis=2, keepdims=True)
        powers = jnp.exp(scores - topmost)
        shares = powers / jnp.sum(powers, axis=2, keepdims=True)
        weights = shares.astype(jnp.bfloat16)
        blended = product("hij,jhd->ihd", weights, value_heads)
        dshares = product("ihd,jhd->hij", grad_heads, value_heads)
        deltas = jnp.sum(grad_heads.astype(jnp.float32) * blended, axis=2)
        dscores = (shares * (dshares - jnp.transpose(deltas)[:, :, None]) * score_scale).astype(
            jnp.bfloat16
        )
        results[0].append(blended.reshape(row_count, group_width))
        results[1].append(
            product("hij,jhd->ihd", dscores, key_heads).reshape(row_count, group_width)
        )
        results[2].append(
            product("hij,ihd->jhd", dscores, query_heads).reshape(
                level_count * row_count, group_width
            )
        )
        results[3].append(
            product("hij,ihd->jhd", weights, grad_heads).reshape(
                level_count * row_count, group_width
            )
        )
    attended = jnp.concatenate(results[0], axis=1).astype(jnp.bfloat16)
    dquery = jnp.concatenate(results[1], axis=1).astype(jnp.bfloat16)
    dkey_rows = jnp.concatenate(results[2], axis=1)
    dvalue_rows = jnp.concatenate(results[3], axis=1)
    return (attended, dquery, dkey_rows, dvalue_rows)


def join_pair(mine, partner, high_bit):
    return jnp.where(
        high_bit == 1,
        jnp.concatenate([partner, mine], axis=1),
        jnp.concatenate([mine, partner], axis=1),
    )


def split_pair(stacked, high_bit):
    halves = stacked.reshape(stacked.shape[0], 2, -1, stacked.shape[-1])
    sending = jnp.where(high_bit == 1, halves[:, 0], halves[:, 1])
    keeping = jnp.where(high_bit == 1, halves[:, 1], halves[:, 0])
    return (sending, keeping)


def on_device(query_vectors, key_vectors, value_vectors, out_grads, offsets):
    row_count, feature_count = query_vectors.shape
    seq_index = lax.axis_index("seq")
    group_index = lax.axis_index("grp")
    seq_size = lax.axis_size("seq")
    span_list = (SPAN_A, seq_size, 4 * seq_size)

    def picked(level_id):
        return jnp.stack(
            [
                select_tiles(key_vectors, offsets[level_id], span_list[level_id]),
                select_tiles(value_vectors, offsets[level_id], span_list[level_id]),
            ]
        )

    near_pair = picked(0)
    for bit_number in (0, 1):
        partner = partner_2(near_pair, "seq", bit_number)
        near_pair = join_pair(near_pair, partner, seq_index >> bit_number & 1)
    wide_pair = lax.all_gather(picked(1), "seq", axis=1, tiled=True)
    outer_pair = picked(2)
    outer_pair = lax.all_gather(outer_pair, "seq", axis=1, tiled=True)
    for bit_number in (0, 1):
        partner = partner_2(outer_pair, "grp", bit_number)
        outer_pair = join_pair(outer_pair, partner, group_index >> bit_number & 1)
    key_rows = jnp.concatenate([key_vectors, near_pair[0], wide_pair[0], outer_pair[0]], axis=0)
    value_rows = jnp.concatenate([value_vectors, near_pair[1], wide_pair[1], outer_pair[1]], axis=0)
    attended, dquery, dkey_rows, dvalue_rows = attend(
        query_vectors, out_grads, key_rows, value_rows
    )

    def level_pair(level_id):
        start_row = level_id * row_count
        return jnp.stack(
            [
                dkey_rows[start_row : start_row + row_count],
                dvalue_rows[start_row : start_row + row_count],
            ]
        )

    near_sum = level_pair(1)
    for bit_number in (1, 0):
        sending, keeping = split_pair(near_sum, seq_index >> bit_number & 1)
        near_sum = keeping + partner_2(sending, "seq", bit_number)
    wide_sum = lax.psum_scatter(level_pair(2), "seq", scatter_dimension=1, tiled=True)
    outer_sum = level_pair(3)
    for bit_number in (1, 0):
        sending, keeping = split_pair(outer_sum, group_index >> bit_number & 1)
        outer_sum = keeping + partner_2(sending, "grp", bit_number)
    outer_sum = lax.psum_scatter(outer_sum, "seq", scatter_dimension=1, tiled=True)
    key_grads = dkey_rows[:row_count]
    value_grads = dvalue_rows[:row_count]
    far_sums = (near_sum, wide_sum, outer_sum)
    for level_id in range(3):
        key_grads = key_grads + spread_rows(
            far_sums[level_id][0], offsets[level_id], span_list[level_id]
        )
        value_grads = value_grads + spread_rows(
            far_sums[level_id][1], offsets[level_id], span_list[level_id]
        )
    return (attended, dquery, key_grads.astype(jnp.bfloat16), value_grads.astype(jnp.bfloat16))


def solution(mesh):
    return jax.shard_map(
        on_device,
        mesh=mesh,
        in_specs=(
            P(("grp", "seq"), None),
            P(("grp", "seq"), None),
            P(("grp", "seq"), None),
            P(("grp", "seq"), None),
            P(),
        ),
        out_specs=(
            P(("grp", "seq"), None),
            P(("grp", "seq"), None),
            P(("grp", "seq"), None),
            P(("grp", "seq"), None),
        ),
        check_vma=False,
    )
```

profile of v0, /device:TPU:56, one launch (start us, length us, event | category | flops | bytes accessed | tf_op | source)
XLA Modules:
  0.0 597.7 jit_solution(3798819941004786982)
XLA Ops:
  7.2 0.8 slice_bitcast_fusion.8
  8.9 1.2 multiply_reduce_fusion.1
  10.2 76.6 %all_gather.7 = bf16[2,32,1024]{2,0,1:T(2,128)(2,1)S(1)} all-gather(bf16[2,1,1024]{2,0,1:T(2,128)(2,1)S(1)} %copy.395), channel_id=1, replica_groups=mesh['grp'=16,'seq'=32] {'seq'}, dimensions={1}, use_global_device_ids=true | all-gather | bytes 135168 | tf_op jit(solution)/shard_map/all_gather | solution.py:138
  87.0 1.9 collective-permute-start.2
  90.6 6.5 %collective-permute-start = (bf16[2,32,1024]{1,2,0:T(8,128)(2,1)S(1)}, bf16[2,32,1024]{1,2,0:T(8,128)(2,1)}, u32[]{:S(2)}, u32[]{:S(2)}) collective-permute-start(bf16[2,32,1024]{1,2,0:T(8,128)(2,1)S(1)} %copy.390), channel_id=1, source_target_pairs={{0,1},{1,0},{2,3},{3,2},{4,5},{5,4},{6,7},{7,6},{8,9},{9,8},{10,11... | collective-permute-start | bytes 393224 | tf_op jit(solution)/shard_map/ppermute | solution.py:20
  98.2 83.3 %all_gather.6 = bf16[2,128,1024]{2,0,1:T(2,128)(2,1)S(1)} all-gather(bf16[2,4,1024]{2,0,1:T(2,128)(2,1)S(1)} %copy.393), channel_id=1, replica_groups=mesh['grp'=16,'seq'=32] {'seq'}, dimensions={1}, use_global_device_ids=true | all-gather | bytes 540672 | tf_op jit(solution)/shard_map/all_gather | solution.py:136
  181.6 0.7 fusion.80
  183.0 1.6 copy.434
  186.1 3.4 collective-permute-start.3
  189.5 1.0 fusion.83
  192.7 0.9 copy.517
  193.6 1.3 dynamic-slice
  195.5 1.8 maximum_select_fusion
  197.3 7.6 %collective-permute-start.1 = (bf16[2,64,1024]{1,2,0:T(8,128)(2,1)S(1)}, bf16[2,64,1024]{1,2,0:T(8,128)(2,1)S(1)}, u32[]{:S(2)}, u32[]{:S(2)}) collective-permute-start(bf16[2,64,1024]{1,2,0:T(8,128)(2,1)S(1)} %maximum_select_fusion), channel_id=1, source_target_pairs={{0,2},{2,0},{1,3},{3,1},{4,6},{6,4},{5,7},{7,5},{8,10},{10,8},{9,1... | collective-permute-start | bytes 786440 | tf_op jit(solution)/shard_map/ppermute | solution.py:20
  205.0 1.8 maximum_select_fusion.3
  206.8 10.7 %collective-permute-done.1 = bf16[2,64,1024]{1,2,0:T(8,128)(2,1)S(1)} collective-permute-done((bf16[2,64,1024]{1,2,0:T(8,128)(2,1)S(1)}, bf16[2,64,1024]{1,2,0:T(8,128)(2,1)S(1)}, u32[]{:S(2)}, u32[]{:S(2)}) %collective-permute-start.1) | collective-permute-done | bytes 262176 | tf_op jit(solution)/shard_map/ppermute | solution.py:20
  218.4 0.9 fusion.79
  219.8 1.2 multiply_reduce_fusion.6
  221.8 0.8 convolution_convert_fusion
  222.7 1.0 fusion.91
  223.9 1.2 fusion.85
  225.1 1.7 multiply_reduce_fusion.7
  227.6 1.2 fusion.86
  228.8 1.8 multiply_reduce_fusion.8
  231.1 1.0 copy.455
  232.1 1.2 fusion.87
  233.3 1.8 multiply_reduce_fusion.9
  235.7 1.0 copy.454
  236.7 1.5 pad_maximum_fusion.1
  238.2 1.0 fusion.77
  239.1 2.1 copy.449
  241.2 1.5 fusion.30
  243.4 1.0 fusion.90
  244.4 2.0 copy.448
  246.4 1.4 fusion.29
  248.6 1.0 fusion.89
  249.6 2.0 copy.447
  251.7 1.4 fusion.28
  253.8 1.0 fusion.88
  254.8 2.1 copy.446
  256.9 1.7 pad_maximum_fusion
  258.9 1.1 copy-done
  260.0 2.4 collective-permute-start.6
  262.5 1.9 collective-permute-start.4
  264.9 6.1 %collective-permute-done.6 = f32[2,64,1024]{2,1,0:T(8,128)S(1)} collective-permute-done((f32[2,64,1024]{2,1,0:T(8,128)S(1)}, f32[2,64,1024]{2,1,0:T(8,128)S(1)}, u32[]{:S(2)}, u32[]{:S(2)}) %collective-permute-start.6) | collective-permute-done | bytes 524320 | tf_op jit(solution)/shard_map/ppermute | solution.py:20
  271.7 1.9 collective-permute-start.7
  273.7 1.1 pad_maximum_fusion.4
  274.7 5.4 collective-permute-done.4
  280.3 0.9 bitcast_add_fusion
  281.2 0.7 select_bitcast_fusion.3
  281.9 1.9 collective-permute-start.5
  284.2 0.9 copy.420
  285.1 0.9 copy.419
  286.1 0.9 copy.418
  287.5 0.7 pad_maximum_fusion.7
  288.2 0.7 pad_maximum_fusion.8
  289.0 1.5 collective-permute-done.5
  290.5 1.0 fusion.45
  291.7 1.0 broadcast_multiply_fusion.1
  292.8 0.9 copy.515
  293.7 292.2 %all-reduce.5.cloned.1.call-done = (f32[2,128,1024]{2,1,0:T(8,128)}, f32[2,32,1024]{2,0,1:T(2,128)}) async-done(((f32[2,128,1024]{2,1,0:T(8,128)}, f32[2,32,1024]{2,0,1:T(2,128)}), (f32[2,128,1024]{2,1,0:T(8,128)}, f32[2,32,1024]{2,0,1:T(2,128)})) %all-reduce.5.cloned.1.call-update) | async-done | bytes 1310736
  585.9 0.8 constant_dynamic-slice_fusion.3
  587.1 1.4 constant_dynamic-slice_fusion.2
  588.6 2.2 fusion.36
  (146 shorter events, 17.5 us)
Async XLA Ops:
  7.2 81.8 %copy-start.2 = (bf16[128,1024]{1,0:T(8,128)(2,1)S(1)}, bf16[128,1024]{1,0:T(8,128)(2,1)}, u32[]{:S(2)}) copy-start(bf16[128,1024]{1,0:T(8,128)(2,1)} %param.6) | copy-start | bytes 786436
  7.2 82.0 %copy-start.1 = (bf16[128,1024]{1,0:T(8,128)(2,1)S(1)}, bf16[128,1024]{1,0:T(8,128)(2,1)}, u32[]{:S(2)}) copy-start(bf16[128,1024]{1,0:T(8,128)(2,1)} %param.7) | copy-start | bytes 786436
  7.2 578.8 %all-reduce.5.cloned.1.call-start = ((), (), s32[]{:S(2)}) async-start(), calls=%async_computation | async-start | bytes 2621440
  87.0 98.4 %collective-permute-start.2 = (bf16[2,32,1024]{1,2,0:T(8,128)(2,1)S(1)}, bf16[2,32,1024]{1,2,0:T(8,128)(2,1)S(1)}, u32[]{:S(2)}, u32[]{:S(2)}) collective-permute-start(bf16[2,32,1024]{1,2,0:T(8,128)(2,1)S(1)} %copy.396), channel_id=1, source_target_pairs={{0,32},{32,0},{64,96},{96,64},{128,160},{160,128},{192,224},{224,1... | collective-permute-start | bytes 393224 | tf_op jit(solution)/shard_map/ppermute | solution.py:20
  90.6 104.9 %collective-permute-start = (bf16[2,32,1024]{1,2,0:T(8,128)(2,1)S(1)}, bf16[2,32,1024]{1,2,0:T(8,128)(2,1)}, u32[]{:S(2)}, u32[]{:S(2)}) collective-permute-start(bf16[2,32,1024]{1,2,0:T(8,128)(2,1)S(1)} %copy.390), channel_id=1, source_target_pairs={{0,1},{1,0},{2,3},{3,2},{4,5},{5,4},{6,7},{7,6},{8,9},{9,8},{10,11... | collective-permute-start | bytes 393224 | tf_op jit(solution)/shard_map/ppermute | solution.py:20
  97.5 84.8 %copy-start.20 = (bf16[128,1024]{1,0:T(8,128)(2,1)S(1)}, bf16[128,1024]{1,0:T(8,128)(2,1)}, u32[]{:S(2)}) copy-start(bf16[128,1024]{1,0:T(8,128)(2,1)} %param.8) | copy-start | bytes 786436
  185.0 5.6 copy-start.21
  185.0 7.5 %copy-start.19 = (f32[128,4]{1,0:T(8,128)S(1)}, f32[128,4]{1,0:T(8,128)}, u32[]{:S(2)}) copy-start(f32[128,4]{1,0:T(8,128)} %get-tuple-element.63) | copy-start | bytes 6148
  186.1 18.9 %collective-permute-start.3 = (bf16[2,64,1024]{1,2,0:T(8,128)(2,1)S(1)}, bf16[2,64,1024]{1,2,0:T(8,128)(2,1)}, u32[]{:S(2)}, u32[]{:S(2)}) collective-permute-start(bf16[2,64,1024]{1,2,0:T(8,128)(2,1)S(1)} %maximum_select_fusion.2), channel_id=1, source_target_pairs={{0,64},{64,0},{32,96},{96,32},{128,192},{192,128},{160,224},{224,1... | collective-permute-start | bytes 786440 | tf_op jit(solution)/shard_map/ppermute | solution.py:20
  190.7 36.2 %copy-start.28 = (bf16[128,256]{0,1:T(8,128)(2,1)}, bf16[128,256]{0,1:T(8,128)(2,1)S(1)}, u32[]{:S(2)}) copy-start(bf16[128,256]{0,1:T(8,128)(2,1)S(1)} %copy.430) | copy-start | bytes 196612
  190.8 36.0 %copy-start.16 = (bf16[128,256]{0,1:T(8,128)(2,1)}, bf16[128,256]{0,1:T(8,128)(2,1)S(1)}, u32[]{:S(2)}) copy-start(bf16[128,256]{0,1:T(8,128)(2,1)S(1)} %copy.509) | copy-start | bytes 196612
  197.3 20.2 %collective-permute-start.1 = (bf16[2,64,1024]{1,2,0:T(8,128)(2,1)S(1)}, bf16[2,64,1024]{1,2,0:T(8,128)(2,1)S(1)}, u32[]{:S(2)}, u32[]{:S(2)}) collective-permute-start(bf16[2,64,1024]{1,2,0:T(8,128)(2,1)S(1)} %maximum_select_fusion), channel_id=1, source_target_pairs={{0,2},{2,0},{1,3},{3,1},{4,6},{6,4},{5,7},{7,5},{8,10},{10,8},{9,1... | collective-permute-start | bytes 786440 | tf_op jit(solution)/shard_map/ppermute | solution.py:20
  218.4 1.4 copy-start.29
  219.3 5.8 copy-start.24
  219.4 7.5 %copy-start.5 = (bf16[512,256]{0,1:T(8,128)(2,1)}, bf16[512,256]{0,1:T(8,128)(2,1)S(1)}, u32[]{:S(2)}) copy-start(bf16[512,256]{0,1:T(8,128)(2,1)S(1)} %get-tuple-element.22) | copy-start | bytes 786436
  219.4 11.2 %copy-start.3 = (bf16[512,256]{0,1:T(8,128)(2,1)}, bf16[512,256]{0,1:T(8,128)(2,1)S(1)}, u32[]{:S(2)}) copy-start(bf16[512,256]{0,1:T(8,128)(2,1)S(1)} %get-tuple-element.23) | copy-start | bytes 786436
  225.1 2.3 copy-start.32
  226.8 2.0 copy-start.23
  226.9 2.0 copy-start.27
  228.8 2.3 copy-start.31
  230.6 2.8 copy-start.22
  230.6 2.8 copy-start.26
  233.3 2.3 copy-start.30
  241.2 2.2 copy-start.17
  242.6 0.7 copy-start.12
  247.9 0.7 copy-start.14
  253.1 0.7 copy-start.10
  258.7 1.4 copy-start
  258.8 5.7 copy-start.6
  258.8 5.7 copy-start.13
  258.8 5.9 copy-start.4
  258.8 5.9 copy-start.15
  260.0 11.1 %collective-permute-start.6 = (f32[2,64,1024]{2,1,0:T(8,128)S(1)}, f32[2,64,1024]{2,1,0:T(8,128)S(1)}, u32[]{:S(2)}, u32[]{:S(2)}) collective-permute-start(f32[2,64,1024]{2,1,0:T(8,128)S(1)} %select_bitcast_fusion), channel_id=1, source_target_pairs={{0,64},{64,0},{32,96},{96,32},{128,192},{192,128},{160,224},{224,1... | collective-permute-start | bytes 1572872 | tf_op jit(solution)/shard_map/ppermute | solution.py:20
  262.5 17.6 %collective-permute-start.4 = (f32[2,64,1024]{2,1,0:T(8,128)S(1)}, f32[2,64,1024]{2,1,0:T(8,128)S(1)}, u32[]{:S(2)}, u32[]{:S(2)}) collective-permute-start(f32[2,64,1024]{2,1,0:T(8,128)S(1)} %select_bitcast_fusion.1), channel_id=1, source_target_pairs={{0,2},{2,0},{1,3},{3,1},{4,6},{6,4},{5,7},{7,5},{8,10},{10,8},{9,1... | collective-permute-start | bytes 1572872 | tf_op jit(solution)/shard_map/ppermute | solution.py:20
  264.9 8.7 %copy-start.7 = (f32[1,128,1024]{2,1,0:T(8,128)S(1)}, f32[1,128,1024]{2,1,0:T(8,128)}, u32[]{:S(2)}) copy-start(f32[1,128,1024]{2,1,0:T(8,128)} %get-tuple-element.17) | copy-start | bytes 1572868
  271.7 8.5 %collective-permute-start.7 = (f32[2,32,1024]{2,0,1:T(2,128)S(1)}, f32[2,32,1024]{2,0,1:T(2,128)S(1)}, u32[]{:S(2)}, u32[]{:S(2)}) collective-permute-start(f32[2,32,1024]{2,0,1:T(2,128)S(1)} %select_bitcast_fusion.2), channel_id=1, source_target_pairs={{0,32},{32,0},{64,96},{96,64},{128,160},{160,128},{192,224},{224,1... | collective-permute-start | bytes 786440 | tf_op jit(solution)/shard_map/ppermute | solution.py:20
  280.2 3.6 copy-start.11
  280.2 3.8 copy-start.25
  280.2 6.8 %copy-start.18 = (bf16[2,128,128]{2,1,0:T(8,128)(2,1)S(1)}, bf16[2,128,128]{2,1,0:T(8,128)(2,1)}, u32[]{:S(2)}) copy-start(bf16[2,128,128]{2,1,0:T(8,128)(2,1)} %convolution_convert_fusion) | copy-start | bytes 196612
  281.9 8.6 %collective-permute-start.5 = (f32[2,32,1024]{2,1,0:T(8,128)}, f32[2,32,1024]{2,1,0:T(8,128)}, u32[]{:S(2)}, u32[]{:S(2)}) collective-permute-start(f32[2,32,1024]{2,1,0:T(8,128)} %select_bitcast_fusion.3), channel_id=1, source_target_pairs={{0,1},{1,0},{2,3},{3,2},{4,5},{5,4},{6,7},{7,6},{8,9},{9,8},{10,11... | collective-permute-start | bytes 786440 | tf_op jit(solution)/shard_map/ppermute | solution.py:20
  292.8 295.8 %copy-start.8 = (f32[16,8,4,256]{3,1,2,0:T(8,128)S(1)}, f32[16,8,4,256]{3,1,2,0:T(8,128)}, u32[]{:S(2)}) copy-start(f32[16,8,4,256]{3,1,2,0:T(8,128)} %copy.517) | copy-start | bytes 1572868
  586.8 1.9 copy-start.9
Sparse Core Ops, SparseCore 0:
  281.3 304.5 all-reduce.4
where the time goes:
time: 604 us; the launch traced here: 598 us
  waiting for transfers between devices  316 us (52%)
  blocking collectives  160 us (26%)
  local copies, waits for them, and re-layouts  35.3 us (6%)
  starting transfers between devices  27.7 us (5%)
  matrix products  22.8 us (4%)
  other arithmetic  20.2 us (3%)
  between operations  15.7 us (3%)
    unnamed x2, waiting for transfers between devices  292 us
    all_gather x1, blocking collectives, on_device(): wide_pair = lax.all_gather(picked(1), 'seq', axis=1, tiled=True)  83.3 us
    all_gather x1, blocking collectives, on_device(): outer_pair = lax.all_gather(outer_pair, 'seq', axis=1, tiled=True)  76.6 us
    ppermute x8, starting transfers between devices, partner_2(): return lax.ppermute(block, axis, route)  27.7 us
    ppermute x8, waiting for transfers between devices, partner_2(): return lax.ppermute(block, axis, route)  23.8 us
    dot_general x20, matrix products, product(): return jnp.einsum(form, left, right, preferred_element_type=jnp.float32)  18.9 us
  transfers between devices with their start and end apart: 9, of which 5 were waited for; matrix products, arithmetic and copies ran while one was open for 5% of the time, Pallas kernels for 0%

commit v1 on v0

v1 whole, which is shorter than its diff:
```python
import math

import jax
import jax.numpy as jnp
from jax import lax
from jax.experimental import pallas as pl
from jax.experimental.pallas import tpu as pltpu
from jax.sharding import PartitionSpec as P

MESH = pl.DeviceIdType.MESH
BF = jnp.bfloat16
F32 = jnp.float32
HD = 128
GROUPS = 4
TOK = 128
WIDTH = 1024
NY = 4
NZ = 8
NE = 4
SCALE = 1.0 / math.sqrt(HD)

Y1, Y2, Y3, Z2, Z3, E3 = 0, 3, 6, 9, 16, 23
FAMILY = 26


def mm(a, b):
    return jnp.dot(a, b, preferred_element_type=F32)


def mm_nt(a, b):
    return lax.dot_general(a, b, (((1,), (1,)), ((), ())), preferred_element_type=F32)


def mm_tn(a, b):
    return lax.dot_general(a, b, (((0,), (0,)), ((), ())), preferred_element_type=F32)


def iotas(shape):
    return (
        lax.broadcasted_iota(jnp.int32, shape, 0),
        lax.broadcasted_iota(jnp.int32, shape, 1),
    )


def onehot(mask):
    return jnp.where(mask, 1.0, 0.0).astype(BF)


def kernel(
    off, q_ref, k_ref, v_ref, do_ref,
    o_ref, dq_ref, dk_ref, dv_ref,
    a1, a2, a3, t3, kv2,
    dkv2, b1s, b1r, b2s, b2r, c2s, c2r, b3s, b3r, c3s, c3r, d3s, d3r,
    dk0, dv0, p2, p2t, p3, p3t,
    send_sem, recv_sem,
):
    grp = lax.axis_index("grp")
    seq = lax.axis_index("seq")
    z = seq // NY
    y = seq % NY

    def y_up(k):
        return (grp, z * NY + (y + k) % NY)

    def y_down(k):
        return (grp, z * NY + (y + NY - k) % NY)

    def z_up(m):
        return (grp, (z + m) % NZ * NY + y)

    def z_down(m):
        return (grp, (z + NZ - m) % NZ * NY + y)

    def partner(e):
        low = grp % NE
        bit0 = (low % 2 + e % 2) % 2
        bit1 = (low // 2 + e // 2) % 2
        return (grp // NE * NE + bit1 * 2 + bit0, seq)

    started = []

    def send(src, dst, index, device):
        copy = pltpu.make_async_remote_copy(
            src_ref=src, dst_ref=dst,
            send_sem=send_sem.at[index], recv_sem=recv_sem.at[index],
            device_id=device, device_id_type=MESH,
        )
        copy.start()
        started.append(copy)
        return copy

    barrier = pltpu.get_barrier_semaphore()
    peers = [y_up(k) for k in range(1, NY)]
    peers += [z_up(m) for m in range(1, NZ)]
    peers += [partner(e) for e in range(1, NE)]
    for peer in peers:
        pl.semaphore_signal(barrier, inc=1, device_id=peer, device_id_type=MESH)

    row, col = iotas((16, TOK))
    acc3 = jnp.zeros((16, HD), F32)
    acc2 = jnp.zeros((16, 512), F32)
    for g in range(GROUPS):
        pick = onehot((row // 4 == g) & (col == 32 * (row % 4) + off[1, g]))
        wide = slice(g * 256, g * 256 + 256)
        both = jnp.concatenate([k_ref[:, wide], v_ref[:, wide]], axis=1)
        acc2 += mm(pick, both)
        for hh in range(2):
            h = 2 * g + hh
            cols = slice(h * HD, h * HD + HD)
            acc3 += mm(onehot((row == h) & (col == off[2, g])), k_ref[:, cols])
            acc3 += mm(onehot((row == 8 + h) & (col == off[2, g])), v_ref[:, cols])
    a3[0, 0] = acc3.astype(BF)
    a2[0, 0] = acc2.astype(BF)
    row, col = iotas((32, TOK))
    for g in range(GROUPS):
        pick = onehot(col == 4 * row + off[0, g])
        wide = slice(g * 256, g * 256 + 256)
        a1[0, 0, :, wide] = mm(pick, k_ref[:, wide]).astype(BF)
        a1[0, 1, :, wide] = mm(pick, v_ref[:, wide]).astype(BF)
    row, col = iotas((512, 512))
    p3[...] = onehot(col == row % 32 * 16 + row // 32)
    p3t[...] = onehot(row == col % 32 * 16 + col // 32)
    p2[...] = onehot(col == row % 128 // 4 * 16 + row // 128 * 4 + row % 4)
    p2t[...] = onehot(row == col % 128 // 4 * 16 + col // 128 * 4 + col % 4)

    pl.semaphore_wait(barrier, len(peers))

    fwd_y3 = [send(a3.at[0, 0], a3.at[0, k], Y3 + k - 1, y_up(k)) for k in range(1, NY)]
    fwd_y2 = [send(a2.at[0, 0], a2.at[0, k], Y2 + k - 1, y_up(k)) for k in range(1, NY)]
    fwd_y1 = [send(a1.at[0], a1.at[k], Y1 + k - 1, y_up(k)) for k in range(1, NY)]
    for copy in fwd_y3:
        copy.wait_recv()
    fwd_z3 = [send(a3.at[0], a3.at[m], Z3 + m - 1, z_up(m)) for m in range(1, NZ)]
    for copy in fwd_y2:
        copy.wait_recv()
    fwd_z2 = [send(a2.at[0], a2.at[m], Z2 + m - 1, z_up(m)) for m in range(1, NZ)]
    for copy in fwd_z3:
        copy.wait_recv()
    t3[0] = mm(p3[...], a3[...].reshape(512, HD)).astype(BF)
    fwd_e3 = [send(t3.at[0], t3.at[e], E3 + e - 1, partner(e)) for e in range(1, NE)]
    for copy in fwd_y1 + fwd_e3 + fwd_z2:
        copy.wait_recv()
    kv2[...] = mm(p2[...], a2[...].reshape(512, 512)).astype(BF)

    for h in range(8):
        g, hh = h // 2, h % 2
        cols = slice(h * HD, h * HD + HD)
        rows2 = slice(g * TOK, g * TOK + TOK)
        kcol2 = slice(hh * HD, hh * HD + HD)
        vcol2 = slice(256 + hh * HD, 256 + hh * HD + HD)
        krow3 = slice(h * 32, h * 32 + 32)
        vrow3 = slice(256 + h * 32, 256 + h * 32 + 32)
        q = q_ref[:, cols]
        do = do_ref[:, cols]
        keys = jnp.concatenate(
            [
                k_ref[:, cols], a1[:, 0, :, cols].reshape(TOK, HD),
                kv2[rows2, kcol2], t3[:, krow3, :].reshape(TOK, HD),
            ],
            axis=0,
        )
        values = jnp.concatenate(
            [
                v_ref[:, cols], a1[:, 1, :, cols].reshape(TOK, HD),
                kv2[rows2, vcol2], t3[:, vrow3, :].reshape(TOK, HD),
            ],
            axis=0,
        )
        scores = mm_nt(q, keys) * SCALE
        powers = jnp.exp(scores - jnp.max(scores, axis=1, keepdims=True))
        shares = powers * (1.0 / jnp.sum(powers, axis=1, keepdims=True))
        weights = shares.astype(BF)
        blended = mm(weights, values)
        dshares = mm_nt(do, values)
        deltas = jnp.sum(do.astype(F32) * blended, axis=1, keepdims=True)
        dscores = (shares * (dshares - deltas) * SCALE).astype(BF)
        o_ref[:, cols] = blended.astype(BF)
        dq_ref[:, cols] = mm(dscores, keys).astype(BF)
        dkeys = mm_tn(dscores, q)
        dvalues = mm_tn(weights, do)
        dk0[:, cols] = dkeys[:TOK]
        dv0[:, cols] = dvalues[:TOK]
        b1s[:, 0, :, cols] = dkeys[TOK : 2 * TOK].reshape(NY, 32, HD).astype(BF)
        b1s[:, 1, :, cols] = dvalues[TOK : 2 * TOK].reshape(NY, 32, HD).astype(BF)
        dkv2[rows2, kcol2] = dkeys[2 * TOK : 3 * TOK].astype(BF)
        dkv2[rows2, vcol2] = dvalues[2 * TOK : 3 * TOK].astype(BF)
        b3s[:, krow3, :] = dkeys[3 * TOK :].reshape(NE, 32, HD).astype(BF)
        b3s[:, vrow3, :] = dvalues[3 * TOK :].reshape(NE, 32, HD).astype(BF)

    back = FAMILY
    bwd_e3 = [send(b3s.at[e], b3r.at[e], back + E3 + e - 1, partner(e)) for e in range(1, NE)]
    b2s[...] = mm(p2t[...], dkv2[...]).astype(BF).reshape(NZ, NY, 16, 512)
    bwd_z2 = [send(b2s.at[m], b2r.at[m], back + Z2 + m - 1, z_down(m)) for m in range(1, NZ)]
    bwd_y1 = [send(b1s.at[k], b1r.at[k], back + Y1 + k - 1, y_down(k)) for k in range(1, NY)]
    for copy in bwd_e3:
        copy.wait_recv()
    total3 = b3s[0].astype(F32)
    for e in range(1, NE):
        total3 += b3r[e].astype(F32)
    c3s[...] = mm(p3t[...], total3.astype(BF)).astype(BF).reshape(NZ, NY, 16, HD)
    bwd_z3 = [send(c3s.at[m], c3r.at[m], back + Z3 + m - 1, z_down(m)) for m in range(1, NZ)]
    for copy in bwd_z2:
        copy.wait_recv()
    total2 = b2s[0].astype(F32)
    for m in range(1, NZ):
        total2 += b2r[m].astype(F32)
    c2s[...] = total2.astype(BF)
    bwd_y2 = [send(c2s.at[k], c2r.at[k], back + Y2 + k - 1, y_down(k)) for k in range(1, NY)]
    for copy in bwd_z3:
        copy.wait_recv()
    total3 = c3s[0].astype(F32)
    for m in range(1, NZ):
        total3 += c3r[m].astype(F32)
    d3s[...] = total3.astype(BF)
    bwd_y3 = [send(d3s.at[k], d3r.at[k], back + Y3 + k - 1, y_down(k)) for k in range(1, NY)]

    for copy in bwd_y1:
        copy.wait_recv()
    b1r[0] = b1s[0]
    for copy in bwd_y2:
        copy.wait_recv()
    c2r[0] = c2s[0]
    for copy in bwd_y3:
        copy.wait_recv()
    sums3 = d3s[0].astype(F32)
    for k in range(1, NY):
        sums3 += d3r[k].astype(F32)
    sums2 = c2r[...].reshape(NY * 16, 512)
    row1, col1 = iotas((TOK, TOK))
    row2, col2 = iotas((TOK, NY * 16))
    row3, _ = iotas((TOK, HD))
    for g in range(GROUPS):
        wide = slice(g * 256, g * 256 + 256)
        place1 = onehot(row1 == 4 * (col1 % 32) + off[0, g])
        place2 = onehot((col2 % 16 // 4 == g) & (row2 == 32 * (col2 % 4) + off[1, g]))
        spread2 = mm(place2, sums2)
        here = row3 == off[2, g]
        for kv, (near, out) in enumerate(((dk0, dk_ref), (dv0, dv_ref))):
            spread3 = jnp.concatenate(
                [
                    jnp.where(here, sums3[kv * 8 + 2 * g + hh][None, :], 0.0)
                    for hh in range(2)
                ],
                axis=1,
            )
            out[:, wide] = (
                near[:, wide]
                + mm(place1, b1r[:, kv, :, wide].reshape(TOK, 256))
                + spread2[:, kv * 256 : kv * 256 + 256]
                + spread3
            ).astype(BF)

    for copy in started:
        copy.wait_send()


def on_device(query_vectors, key_vectors, value_vectors, out_grads, offsets):
    vmem = pl.BlockSpec(memory_space=pltpu.VMEM)
    shape = jax.ShapeDtypeStruct((TOK, WIDTH), BF)
    half = lambda *dims: pltpu.VMEM(dims, BF)
    return pl.pallas_call(
        kernel,
        out_shape=(shape,) * 4,
        in_specs=[pl.BlockSpec(memory_space=pltpu.SMEM)] + [vmem] * 4,
        out_specs=(vmem,) * 4,
        scratch_shapes=[
            half(NY, 2, 32, WIDTH),
            half(NZ, NY, 16, 512),
            half(NZ, NY, 16, HD),
            half(NE, 512, HD),
            half(512, 512),
            half(512, 512),
            half(NY, 2, 32, WIDTH),
            half(NY, 2, 32, WIDTH),
            half(NZ, NY, 16, 512),
            half(NZ, NY, 16, 512),
            half(NY, 16, 512),
            half(NY, 16, 512),
            half(NE, 512, HD),
            half(NE, 512, HD),
            half(NZ, NY, 16, HD),
            half(NZ, NY, 16, HD),
            half(NY, 16, HD),
            half(NY, 16, HD),
            pltpu.VMEM((TOK, WIDTH), F32),
            pltpu.VMEM((TOK, WIDTH), F32),
            half(512, 512),
            half(512, 512),
            half(512, 512),
            half(512, 512),
            pltpu.SemaphoreType.DMA((2 * FAMILY,)),
            pltpu.SemaphoreType.DMA((2 * FAMILY,)),
        ],
        compiler_params=pltpu.CompilerParams(
            collective_id=0, has_side_effects=True, vmem_limit_bytes=40 * 1024 * 1024
        ),
        cost_estimate=pl.CostEstimate(
            flops=1_500_000_000, bytes_accessed=2 * 1024 * 1024, transcendentals=524288
        ),
    )(offsets, query_vectors, key_vectors, value_vectors, out_grads)


def solution(mesh):
    rows = P(("grp", "seq"), None)
    return jax.shard_map(
        on_device,
        mesh=mesh,
        in_specs=(rows, rows, rows, rows, P()),
        out_specs=(rows,) * 4,
        check_vma=False,
    )
```

time: 604 us -> 67.7 us (0.11)
  waiting for transfers between devices: 316 us -> 0 us
  blocking collectives: 160 us -> 0 us
  Pallas kernels: 0 us -> 58.5 us
  local copies, waits for them, and re-layouts: 35.3 us -> 7.28 us
  starting transfers between devices: 27.7 us -> 0 us
  matrix products: 22.8 us -> 0 us
  other arithmetic: 20.2 us -> 0 us
  between operations: 15.7 us -> 0.65 us
    unnamed x2 -> x0, waiting for transfers between devices: 292 us -> none
    all_gather x2 -> x0, blocking collectives: 160 us -> none  [the longest x1 83.3 us: on_device(): wide_pair = lax.all_gather(picked(1), 'seq', axis=1, tiled=True)]
    pallas_call x0 -> x1, Pallas kernels: none -> 58.5 us  [on_device(): pl.pallas_call(kernel, out_shape=(shape,) * 4, in_specs=[pl.BlockSpec(mem...]
    ppermute x8 -> x0, starting transfers between devices: 27.7 us -> none  [partner_2(): return lax.ppermute(block, axis, route)]
    ppermute x8 -> x0, waiting for transfers between devices: 23.8 us -> none  [partner_2(): return lax.ppermute(block, axis, route)]
    dot_general x20 -> x0, matrix products: 18.9 us -> none  [product(): return jnp.einsum(form, left, right, preferred_element_type=jnp.float32)]
    reshape x20 -> x0, local copies, waits for them, and re-layouts: 14.7 us -> none  [the longest x4 8.17 us: attend(): product('hij,ihd->jhd', dscores, query_heads)]
    slice x14 -> x0, local copies, waits for them, and re-layouts: 9.71 us -> none  [the longest x5 3.79 us: attend(): grads[:, start_col:start_col + group_width]]
  transfers between devices with their start and end apart: 9 -> 0, of which waited for: 5 -> 0; matrix products, arithmetic and copies ran while one was open for 5% -> 0% of each run, Pallas kernels for 0% -> 0%
where the time goes in v1:
time: 67.7 us; the launch traced here: 66.5 us
  Pallas kernels  58.5 us (86%)
  local copies, waits for them, and re-layouts  7.28 us (11%)
    pallas_call x1, Pallas kernels, on_device(): pl.pallas_call(kernel, out_shape=(shape,) * 4, in_specs=[pl.BlockSpec(mem...  58.5 us
    unnamed x14, local copies, waits for them, and re-layouts  7.28 us

profile of v1, /device:TPU:56, one launch (start us, length us, event | category | flops | bytes accessed | tf_op | source)
XLA Modules:
  0.0 66.5 jit_solution(6003857741913081643)
XLA Ops:
  0.6 0.0 copy-start
  0.6 0.9 %copy-done = bf16[128,1024]{1,0:T(8,128)(2,1)S(1)} copy-done((bf16[128,1024]{1,0:T(8,128)(2,1)S(1)}, bf16[128,1024]{1,0:T(8,128)(2,1)}, u32[]{:S(2)}) %copy-start) | copy-done | bytes 262168
  1.6 0.0 copy-start.1
  1.6 0.9 %copy-done.1 = bf16[128,1024]{1,0:T(8,128)(2,1)S(1)} copy-done((bf16[128,1024]{1,0:T(8,128)(2,1)S(1)}, bf16[128,1024]{1,0:T(8,128)(2,1)}, u32[]{:S(2)}) %copy-start.1) | copy-done | bytes 262168
  2.5 0.0 copy-start.2
  2.5 0.9 %copy-done.2 = bf16[128,1024]{1,0:T(8,128)(2,1)S(1)} copy-done((bf16[128,1024]{1,0:T(8,128)(2,1)S(1)}, bf16[128,1024]{1,0:T(8,128)(2,1)}, u32[]{:S(2)}) %copy-start.2) | copy-done | bytes 262168
  3.5 0.0 copy-start.3
  3.5 0.9 %copy-done.3 = bf16[128,1024]{1,0:T(8,128)(2,1)S(1)} copy-done((bf16[128,1024]{1,0:T(8,128)(2,1)S(1)}, bf16[128,1024]{1,0:T(8,128)(2,1)}, u32[]{:S(2)}) %copy-start.3) | copy-done | bytes 262168
  4.4 0.0 copy-start.4
  4.4 0.7 %copy-done.4 = s32[3,4]{1,0:T(4,128)S(1)} copy-done((s32[3,4]{1,0:T(4,128)S(1)}, s32[3,4]{1,0:T(4,128)}, u32[]{:S(2)}) %copy-start.4) | copy-done | bytes 72
  5.1 58.5 %shard_map.84 = (bf16[128,1024]{1,0:T(8,128)(2,1)S(1)}, bf16[128,1024]{1,0:T(8,128)(2,1)S(1)}, bf16[128,1024]{1,0:T(8,128)(2,1)S(1)}, bf16[128,1024]{1,0:T(8,128)(2,1)S(1)}) custom-call(s32[3,4]{1,0:T(4,128)S(1)} %copy-done.4, bf16[128,1024]{1,0:T(8,128)(2,1)S(1)} %copy-done, bf16[128,1024]{1,0:T(8,128)(2,1)S(1)} %copy-done.1, ...), custom_call_target="tpu_custom_call" | custom-call | flops 1500000000 | bytes 2097152 | tf_op jit(solution)/shard_map/pallas_call | solution.py:261
  63.7 0.7 %copy.13 = bf16[128,1024]{1,0:T(8,128)(2,1)} copy(bf16[128,1024]{1,0:T(8,128)(2,1)S(1)} %get-tuple-element.8) | data formatting | bytes 524288
  64.4 0.7 %copy.14 = bf16[128,1024]{1,0:T(8,128)(2,1)} copy(bf16[128,1024]{1,0:T(8,128)(2,1)S(1)} %get-tuple-element.9) | data formatting | bytes 524288
  65.1 0.7 %copy.15 = bf16[128,1024]{1,0:T(8,128)(2,1)} copy(bf16[128,1024]{1,0:T(8,128)(2,1)S(1)} %get-tuple-element.10) | data formatting | bytes 524288
  65.8 0.7 %copy.16 = bf16[128,1024]{1,0:T(8,128)(2,1)} copy(bf16[128,1024]{1,0:T(8,128)(2,1)S(1)} %get-tuple-element.11) | data formatting | bytes 524288
Async XLA Ops:
  0.6 1.0 %copy-start = (bf16[128,1024]{1,0:T(8,128)(2,1)S(1)}, bf16[128,1024]{1,0:T(8,128)(2,1)}, u32[]{:S(2)}) copy-start(bf16[128,1024]{1,0:T(8,128)(2,1)} %q_ref.1) | copy-start | bytes 786436
  1.6 0.9 %copy-start.1 = (bf16[128,1024]{1,0:T(8,128)(2,1)S(1)}, bf16[128,1024]{1,0:T(8,128)(2,1)}, u32[]{:S(2)}) copy-start(bf16[128,1024]{1,0:T(8,128)(2,1)} %k_ref.1) | copy-start | bytes 786436
  2.5 0.9 %copy-start.2 = (bf16[128,1024]{1,0:T(8,128)(2,1)S(1)}, bf16[128,1024]{1,0:T(8,128)(2,1)}, u32[]{:S(2)}) copy-start(bf16[128,1024]{1,0:T(8,128)(2,1)} %v_ref.1) | copy-start | bytes 786436
  3.5 0.9 %copy-start.3 = (bf16[128,1024]{1,0:T(8,128)(2,1)S(1)}, bf16[128,1024]{1,0:T(8,128)(2,1)}, u32[]{:S(2)}) copy-start(bf16[128,1024]{1,0:T(8,128)(2,1)} %do_ref.1) | copy-start | bytes 786436
  4.4 0.7 %copy-start.4 = (s32[3,4]{1,0:T(4,128)S(1)}, s32[3,4]{1,0:T(4,128)}, u32[]{:S(2)}) copy-start(s32[3,4]{1,0:T(4,128)} %off.1) | copy-start | bytes 148

commit v2 on v1

v2 whole, which is shorter than its diff:
```python
import math

import jax
import jax.numpy as jnp
from jax import lax
from jax.experimental import pallas as pl
from jax.experimental.pallas import tpu as pltpu
from jax.sharding import PartitionSpec as P

MESH = pl.DeviceIdType.MESH
BF = jnp.bfloat16
F32 = jnp.float32
HD = 128
GROUPS = 4
TOK = 128
WIDTH = 1024
NY = 4
NZ = 8
NE = 4
SCALE = 1.0 / math.sqrt(HD)

Y3, Y2, Y1, Z3, Z2, E3 = 0, 3, 6, 18, 25, 57
FAMILY = 69


def mm(a, b):
    return jnp.dot(a, b, preferred_element_type=F32)


def mm_nt(a, b):
    return lax.dot_general(a, b, (((1,), (1,)), ((), ())), preferred_element_type=F32)


def mm_tn(a, b):
    return lax.dot_general(a, b, (((0,), (0,)), ((), ())), preferred_element_type=F32)


def iotas(shape):
    return (
        lax.broadcasted_iota(jnp.int32, shape, 0),
        lax.broadcasted_iota(jnp.int32, shape, 1),
    )


def onehot(mask):
    return jnp.where(mask, 1.0, 0.0).astype(BF)


def exchange(
    off_hbm, q_hbm, k_hbm, v_hbm, do_hbm,
    o_ref, dq_ref, dk_ref, dv_ref,
    off, q_ref, k_ref, v_ref, do_ref,
    a1, a2, a3, t3,
    b1s, b1r, b2s, b2r, b2t, c2s, c2r, b3s, b3r, c3s, c3r, d3s, d3r,
    dk0, dv0, p2, p2t, p3, p3t, place1, place2,
    load_sem, send_sem, recv_sem,
):
    grp = lax.axis_index("grp")
    seq = lax.axis_index("seq")
    z = seq // NY
    y = seq % NY

    def at_y(k):
        return (grp, z * NY + (y + k + NY) % NY)

    def at_z(m):
        return (grp, (z + m + NZ) % NZ * NY + y)

    def partner(e):
        low = grp % NE
        bit0 = (low % 2 + e % 2) % 2
        bit1 = (low // 2 + e // 2) % 2
        return (grp // NE * NE + bit1 * 2 + bit0, seq)

    barrier = pltpu.get_barrier_semaphore()
    peers = [at_y(k) for k in range(1, NY)]
    peers += [at_z(m) for m in range(1, NZ)]
    peers += [partner(e) for e in range(1, NE)]
    for peer in peers:
        pl.semaphore_signal(barrier, inc=1, device_id=peer, device_id_type=MESH)

    loads = [
        pltpu.make_async_copy(src, dst, load_sem.at[i])
        for i, (src, dst) in enumerate(
            ((off_hbm, off), (k_hbm, k_ref), (v_hbm, v_ref), (q_hbm, q_ref), (do_hbm, do_ref))
        )
    ]
    for load in loads:
        load.start()

    started = []

    def send(src, dst, index, device):
        copy = pltpu.make_async_remote_copy(
            src_ref=src, dst_ref=dst,
            send_sem=send_sem.at[index], recv_sem=recv_sem.at[index],
            device_id=device, device_id_type=MESH,
        )
        copy.start()
        started.append(copy)
        return copy

    row, col = iotas((512, 512))
    p3[...] = onehot(col == row % 32 * 16 + row % 128 // 64 * 8 + row // 128 * 2 + row % 64 // 32)
    p2[...] = onehot(col == row % 128 // 4 * 16 + row // 128 * 4 + row % 4)

    for load in loads[:3]:
        load.wait()
    row, col = iotas((32, TOK))
    acc3 = jnp.zeros((16, HD), F32)
    for g in range(GROUPS):
        acc2 = jnp.zeros((16, HD), F32)
        for c in range(4):
            kv, hh = c // 2, c % 2
            h = 2 * g + hh
            source = (k_ref, v_ref)[kv]
            pick = onehot(
                ((row // 4 == c) & (col == 32 * (row % 4) + off[1, g]))
                | ((row == 16 + kv * 8 + h) & (col == off[2, g]))
            )
            rows = mm(pick, source[:, h * HD : h * HD + HD])
            acc2 += rows[:16]
            acc3 += rows[16:]
        a2[0, g, 0] = acc2.astype(BF)
    a3[0, 0] = acc3.astype(BF)

    pl.semaphore_wait(barrier, len(peers))

    fwd_y3 = [send(a3.at[0, 0], a3.at[0, k], Y3 + k - 1, at_y(k)) for k in range(1, NY)]
    fwd_y2 = [send(a2.at[0, :, 0], a2.at[0, :, k], Y2 + k - 1, at_y(k)) for k in range(1, NY)]
    row, col = iotas((32, TOK))
    fwd_y1 = []
    for g in range(GROUPS):
        pick = onehot(col == 4 * row + off[0, g])
        wide = slice(g * 256, g * 256 + 256)
        a1[0, g, 0] = mm(pick, k_ref[:, wide]).astype(BF)
        a1[0, g, 1] = mm(pick, v_ref[:, wide]).astype(BF)
        fwd_y1.append(
            [send(a1.at[0, g], a1.at[k, g], Y1 + g * 3 + k - 1, at_y(k)) for k in range(1, NY)]
        )

    for copy in fwd_y3:
        copy.wait_recv()
    fwd_z3 = [send(a3.at[0], a3.at[m], Z3 + m - 1, at_z(m)) for m in range(1, NZ)]
    for copy in fwd_y2:
        copy.wait_recv()
    fwd_z2 = []
    for g in range(GROUPS):
        base = Z2 + g * 8
        fwd_z2.append(
            [
                send(a2.at[0, g], a2.at[2, g], base, at_z(2)),
                send(a2.at[0, g], a2.at[6, g], base + 1, at_z(-2)),
                send(a2.at[0, g], a2.at[1, g], base + 2, at_z(1)),
                send(a2.at[0, g], a2.at[7, g], base + 3, at_z(-1)),
            ]
        )

    row, col = iotas((512, 512))
    p3t[...] = onehot(row == col % 32 * 16 + col % 128 // 64 * 8 + col // 128 * 2 + col % 64 // 32)
    p2t[...] = onehot(row == col % 128 // 4 * 16 + col // 128 * 4 + col % 4)
    row1, col1 = iotas((TOK, TOK))
    row2, col2 = iotas((512, NY * 16))
    for g in range(GROUPS):
        place1[g] = onehot(row1 == 4 * (col1 % 32) + off[0, g])
        place2[g] = onehot(
            (col2 % 16 // 4 == row2 // 128) & (row2 % 128 == 32 * (col2 % 4) + off[1, g])
        )
    for load in loads[3:]:
        load.wait()

    for copy in fwd_z3:
        copy.wait_recv()
    t3[0] = mm(p3[...], a3[...].reshape(512, HD)).astype(BF).reshape(GROUPS, TOK, HD)
    fwd_e3 = []
    for g in range(GROUPS):
        fwd_e3.append(
            [send(t3.at[0, g], t3.at[e, g], E3 + g * 3 + e - 1, partner(e)) for e in range(1, NE)]
        )
    half = pl.ds(0, 2)
    rest = pl.ds(2, 2)
    for g in range(GROUPS):
        base = Z2 + g * 8
        fwd_z2[g][0].wait_recv()
        fwd_z2[g][1].wait_recv()
        fwd_z2[g] = fwd_z2[g][2:] + [
            send(a2.at[2, g], a2.at[3, g], base + 4, at_z(1)),
            send(a2.at[6, g], a2.at[5, g], base + 5, at_z(-1)),
            send(a2.at[2, g, half], a2.at[4, g, half], base + 6, at_z(2)),
            send(a2.at[6, g, rest], a2.at[4, g, rest], base + 7, at_z(-2)),
        ]

    back = FAMILY
    bwd_e3, bwd_z2, bwd_y1 = [], [], []
    for g in range(GROUPS):
        for copy in fwd_y1[g] + fwd_z2[g] + fwd_e3[g]:
            copy.wait_recv()
        tile2 = mm(p2[...], a2[:, g].reshape(512, HD)).astype(BF)
        grads2 = [None] * 4
        for hh in range(2):
            h = 2 * g + hh
            cols = slice(h * HD, h * HD + HD)
            part = slice(hh * HD, hh * HD + HD)
            krow3 = slice(hh * 32, hh * 32 + 32)
            vrow3 = slice(64 + hh * 32, 64 + hh * 32 + 32)
            q = q_ref[:, cols]
            do = do_ref[:, cols]
            keys = jnp.concatenate(
                [
                    k_ref[:, cols],
                    a1[:, g, 0, :, part].reshape(TOK, HD),
                    tile2[hh * TOK : hh * TOK + TOK],
                    t3[:, g, krow3, :].reshape(TOK, HD),
                ],
                axis=0,
            )
            values = jnp.concatenate(
                [
                    v_ref[:, cols],
                    a1[:, g, 1, :, part].reshape(TOK, HD),
                    tile2[256 + hh * TOK : 256 + hh * TOK + TOK],
                    t3[:, g, vrow3, :].reshape(TOK, HD),
                ],
                axis=0,
            )
            scores = mm_nt(q, keys) * SCALE
            powers = jnp.exp(scores - jnp.max(scores, axis=1, keepdims=True))
            shares = powers * (1.0 / jnp.sum(powers, axis=1, keepdims=True))
            weights = shares.astype(BF)
            blended = mm(weights, values)
            dshares = mm_nt(do, values)
            deltas = jnp.sum(do.astype(F32) * blended, axis=1, keepdims=True)
            dscores = (shares * (dshares - deltas) * SCALE).astype(BF)
            dkeys = mm_tn(dscores, q)
            dvalues = mm_tn(weights, do)
            b3s[:, g, krow3, :] = dkeys[3 * TOK :].reshape(NE, 32, HD).astype(BF)
            b3s[:, g, vrow3, :] = dvalues[3 * TOK :].reshape(NE, 32, HD).astype(BF)
            b1s[:, g, 0, :, part] = dkeys[TOK : 2 * TOK].reshape(NY, 32, HD).astype(BF)
            b1s[:, g, 1, :, part] = dvalues[TOK : 2 * TOK].reshape(NY, 32, HD).astype(BF)
            grads2[hh] = dkeys[2 * TOK : 3 * TOK].astype(BF)
            grads2[2 + hh] = dvalues[2 * TOK : 3 * TOK].astype(BF)
            dk0[:, cols] = dkeys[:TOK]
            dv0[:, cols] = dvalues[:TOK]
            o_ref[:, cols] = blended.astype(BF)
            dq_ref[:, cols] = mm(dscores, keys).astype(BF)
        bwd_e3.append(
            [
                send(b3s.at[e, g], b3r.at[e, g], back + E3 + g * 3 + e - 1, partner(e))
                for e in range(1, NE)
            ]
        )
        bwd_y1.append(
            [
                send(b1s.at[k, g], b1r.at[k, g], back + Y1 + g * 3 + k - 1, at_y(-k))
                for k in range(1, NY)
            ]
        )
        b2s[:, g] = (
            mm(p2t[...], jnp.concatenate(grads2, axis=0)).astype(BF).reshape(NZ, NY, 16, HD)
        )
        base = back + Z2 + g * 8
        bwd_z2.append(
            [
                send(b2s.at[4, g, half], b2r.at[4, g, half], base, at_z(-2)),
                send(b2s.at[4, g, rest], b2r.at[4, g, rest], base + 1, at_z(2)),
                send(b2s.at[3, g], b2r.at[3, g], base + 2, at_z(-1)),
                send(b2s.at[5, g], b2r.at[5, g], base + 3, at_z(1)),
                send(b2s.at[1, g], b2r.at[1, g], base + 4, at_z(-1)),
                send(b2s.at[7, g], b2r.at[7, g], base + 5, at_z(1)),
            ]
        )

    def relay(g):
        for copy in bwd_z2[g][:4]:
            copy.wait_recv()
        base = back + Z2 + g * 8
        low = b2s[2, g].astype(F32) + b2r[3, g].astype(F32)
        high = b2s[6, g].astype(F32) + b2r[5, g].astype(F32)
        b2t[0, g, half] = (low[:2] + b2r[4, g, half].astype(F32)).astype(BF)
        b2t[0, g, rest] = low[2:].astype(BF)
        b2t[1, g, half] = high[:2].astype(BF)
        b2t[1, g, rest] = (high[2:] + b2r[4, g, rest].astype(F32)).astype(BF)
        bwd_z2[g] = bwd_z2[g][4:] + [
            send(b2t.at[0, g], b2r.at[2, g], base + 6, at_z(-2)),
            send(b2t.at[1, g], b2r.at[6, g], base + 7, at_z(2)),
        ]

    relay(0)
    relay(1)
    for copies in bwd_e3:
        for copy in copies:
            copy.wait_recv()
    total3 = b3s[0].astype(F32)
    for e in range(1, NE):
        total3 += b3r[e].astype(F32)
    c3s[...] = (
        mm(p3t[...], total3.astype(BF).reshape(512, HD)).astype(BF).reshape(NZ, NY, 16, HD)
    )
    bwd_z3 = [send(c3s.at[m], c3r.at[m], back + Z3 + m - 1, at_z(-m)) for m in range(1, NZ)]
    relay(2)
    relay(3)
    count = len(started)
    for g in range(GROUPS):
        for copy in bwd_y1[g]:
            copy.wait_recv()
        wide = slice(g * 256, g * 256 + 256)
        for kv, near in enumerate((dk0, dv0)):
            sums1 = jnp.concatenate([b1s[0, g, kv], b1r[1:, g, kv].reshape(96, 256)], axis=0)
            near[:, wide] += mm(place1[g], sums1)
    for g in range(GROUPS):
        for copy in bwd_z2[g]:
            copy.wait_recv()
        total2 = b2s[0, g].astype(F32)
        for m in (1, 2, 6, 7):
            total2 += b2r[m, g].astype(F32)
        c2s[:, g] = total2.astype(BF)
    bwd_y2 = [send(c2s.at[k], c2r.at[k], back + Y2 + k - 1, at_y(-k)) for k in range(1, NY)]
    for copy in bwd_z3:
        copy.wait_recv()
    total3 = c3s[0].astype(F32)
    for m in range(1, NZ):
        total3 += c3r[m].astype(F32)
    d3s[...] = total3.astype(BF)
    bwd_y3 = [send(d3s.at[k], d3r.at[k], back + Y3 + k - 1, at_y(-k)) for k in range(1, NY)]

    for copy in started[:count]:
        copy.wait_send()
    for copy in bwd_y2:
        copy.wait_recv()
    for g in range(GROUPS):
        sums2 = jnp.concatenate([c2s[0, g], c2r[1:, g].reshape(48, HD)], axis=0)
        spread2 = mm(place2[g], sums2)
        for hh in range(2):
            cols = slice((2 * g + hh) * HD, (2 * g + hh) * HD + HD)
            dk0[:, cols] += spread2[hh * TOK : hh * TOK + TOK]
            dv0[:, cols] += spread2[256 + hh * TOK : 256 + hh * TOK + TOK]
    for copy in bwd_y3:
        copy.wait_recv()
    sums3 = d3s[0].astype(F32)
    for k in range(1, NY):
        sums3 += d3r[k].astype(F32)
    row3, _ = iotas((TOK, HD))
    for h in range(8):
        cols = slice(h * HD, h * HD + HD)
        here = row3 == off[2, h // 2]
        dk_ref[:, cols] = (dk0[:, cols] + jnp.where(here, sums3[h][None, :], 0.0)).astype(BF)
        dv_ref[:, cols] = (dv0[:, cols] + jnp.where(here, sums3[8 + h][None, :], 0.0)).astype(BF)

    for copy in started[count:]:
        copy.wait_send()


def write_out(*refs):
    sources, targets, held, load_sem, store_sem = refs[:4], refs[4:8], refs[8], refs[9], refs[10]
    loads = [
        pltpu.make_async_copy(src, held.at[i], load_sem.at[i]) for i, src in enumerate(sources)
    ]
    stores = [
        pltpu.make_async_copy(held.at[i], dst, store_sem.at[i]) for i, dst in enumerate(targets)
    ]
    for load in loads:
        load.start()
    for load, store in zip(loads, stores):
        load.wait()
        store.start()
    for store in stores:
        store.wait()


def on_device(query_vectors, key_vectors, value_vectors, out_grads, offsets):
    vmem = pl.BlockSpec(memory_space=pltpu.VMEM)
    anywhere = pl.BlockSpec(memory_space=pl.ANY)
    shape = jax.ShapeDtypeStruct((TOK, WIDTH), BF)
    half = lambda *dims: pltpu.VMEM(dims, BF)
    results = pl.pallas_call(
        exchange,
        out_shape=(shape,) * 4,
        in_specs=[anywhere] * 5,
        out_specs=(vmem,) * 4,
        scratch_shapes=[
            pltpu.SMEM((3, GROUPS), jnp.int32),
            half(TOK, WIDTH),
            half(TOK, WIDTH),
            half(TOK, WIDTH),
            half(TOK, WIDTH),
            half(NY, GROUPS, 2, 32, 256),
            half(NZ, GROUPS, NY, 16, HD),
            half(NZ, NY, 16, HD),
            half(NE, GROUPS, TOK, HD),
            half(NY, GROUPS, 2, 32, 256),
            half(NY, GROUPS, 2, 32, 256),
            half(NZ, GROUPS, NY, 16, HD),
            half(NZ, GROUPS, NY, 16, HD),
            half(2, GROUPS, NY, 16, HD),
            half(NY, GROUPS, 16, HD),
            half(NY, GROUPS, 16, HD),
            half(NE, GROUPS, TOK, HD),
            half(NE, GROUPS, TOK, HD),
            half(NZ, NY, 16, HD),
            half(NZ, NY, 16, HD),
            half(NY, 16, HD),
            half(NY, 16, HD),
            pltpu.VMEM((TOK, WIDTH), F32),
            pltpu.VMEM((TOK, WIDTH), F32),
            half(512, 512),
            half(512, 512),
            half(512, 512),
            half(512, 512),
            half(GROUPS, TOK, TOK),
            half(GROUPS, 512, NY * 16),
            pltpu.SemaphoreType.DMA((5,)),
            pltpu.SemaphoreType.DMA((2 * FAMILY,)),
            pltpu.SemaphoreType.DMA((2 * FAMILY,)),
        ],
        compiler_params=pltpu.CompilerParams(
            collective_id=0, has_side_effects=True, vmem_limit_bytes=56 * 1024 * 1024
        ),
        cost_estimate=pl.CostEstimate(
            flops=1_500_000_000, bytes_accessed=2 * 1024 * 1024, transcendentals=524288
        ),
    )(offsets, query_vectors, key_vectors, value_vectors, out_grads)
    return pl.pallas_call(
        write_out,
        out_shape=(shape,) * 4,
        in_specs=[anywhere] * 4,
        out_specs=(anywhere,) * 4,
        scratch_shapes=[
            half(4, TOK, WIDTH),
            pltpu.SemaphoreType.DMA((4,)),
            pltpu.SemaphoreType.DMA((4,)),
        ],
        compiler_params=pltpu.CompilerParams(vmem_limit_bytes=60 * 1024 * 1024),
        cost_estimate=pl.CostEstimate(
            flops=0, bytes_accessed=2 * 1024 * 1024, transcendentals=0
        ),
    )(*results)


def solution(mesh):
    rows = P(("grp", "seq"), None)
    return jax.shard_map(
        on_device,
        mesh=mesh,
        in_specs=(rows, rows, rows, rows, P()),
        out_specs=(rows,) * 4,
        check_vma=False,
    )
```

time: 67.7 us -> 56.6 us (0.84)
  the two profiles are of different devices: /device:TPU:56 before, /device:TPU:1 now
where the time goes in v2:
time: 56.6 us; the launch traced here: 56.4 us
  Pallas kernels  55.8 us (99%)
  between operations  0.64 us (1%)
    pallas_call x1, Pallas kernels, on_device(): pl.pallas_call(exchange, out_shape=(shape,) * 4, in_specs=[anywhere] * 5,...  53.8 us
    pallas_call x1, Pallas kernels, on_device(): pl.pallas_call(write_out, out_shape=(shape,) * 4, in_specs=[anywhere] * 4...  1.98 us

profile of v2, /device:TPU:1, one launch (start us, length us, event | category | flops | bytes accessed | tf_op | source)
XLA Modules:
  0.0 56.4 jit_solution(10156522155982029018)
XLA Ops:
  0.6 53.8 %shard_map.84 = (bf16[128,1024]{1,0:T(8,128)(2,1)}, bf16[128,1024]{1,0:T(8,128)(2,1)}, bf16[128,1024]{1,0:T(8,128)(2,1)}, bf16[128,1024]{1,0:T(8,128)(2,1)}) custom-call(s32[3,4]{1,0:T(4,128)} %off_hbm.1, bf16[128,1024]{1,0:T(8,128)(2,1)} %q_hbm.1, bf16[128,1024]{1,0:T(8,128)(2,1)} %k_hbm.1, bf16[128,1024]{1,0:T(8,128)(2,1)} %v_hbm.1, bf16[128,1024]{1,0:T(8,128)(2,1)} %do_hbm.1), custom_call_target="tpu_custom_call" | custom-call | flops 1500000000 | bytes 2097152 | tf_op jit(solution)/shard_map/pallas_call | solution.py:375
  54.4 2.0 %shard_map.85 = (bf16[128,1024]{1,0:T(8,128)(2,1)}, bf16[128,1024]{1,0:T(8,128)(2,1)}, bf16[128,1024]{1,0:T(8,128)(2,1)}, bf16[128,1024]{1,0:T(8,128)(2,1)}) custom-call(bf16[128,1024]{1,0:T(8,128)(2,1)} %get-tuple-element.8.refs_0_, bf16[128,1024]{1,0:T(8,128)(2,1)} %get-tuple-element.9.refs_1_, bf16[128,1024]{1,0:T(8,128)(2,1)} %get-tuple-element.10.refs_2_, ...), custom_call_target="tpu_custom_call" | custom-call | bytes 2097152 | tf_op jit(solution)/shard_map/pallas_call | solution.py:422

commit v3 on v2

--- a/solution.py
+++ b/solution.py
@@ -19,8 +19,11 @@
 NE = 4
 SCALE = 1.0 / math.sqrt(HD)
 
-Y3, Y2, Y1, Z3, Z2, E3 = 0, 3, 6, 18, 25, 57
-FAMILY = 69
+S3, Y2, Y1, Z2, E3 = 0, 32, 35, 47, 79
+FAMILY = 91
+DIRECT_F = (0, 1, 2, 3)
+DIRECT_B = ()
+OTHERS = [(m, k) for m in (4, 3, 5, 2, 6, 1, 7, 0) for k in (3, 2, 1, 0) if (m, k) != (0, 0)]
 
 
 def mm(a, b):
@@ -50,9 +53,9 @@
     off_hbm, q_hbm, k_hbm, v_hbm, do_hbm,
     o_ref, dq_ref, dk_ref, dv_ref,
     off, q_ref, k_ref, v_ref, do_ref,
-    a1, a2, a3, t3,
-    b1s, b1r, b2s, b2r, b2t, c2s, c2r, b3s, b3r, c3s, c3r, d3s, d3r,
-    dk0, dv0, p2, p2t, p3, p3t, place1, place2,
+    a1, a2, a3, t3, kv2, kept_w, kept_d,
+    b1s, b1r, b2s, b2r, b2t, c2s, c2r, b3s, b3r, c3s, c3r,
+    own_s, own_d, dk0, dv0, p2, p2t, p3, p3t, place1, place2,
     load_sem, send_sem, recv_sem,
 ):
     grp = lax.axis_index("grp")
@@ -66,19 +69,15 @@
     def at_z(m):
         return (grp, (z + m + NZ) % NZ * NY + y)
 
+    def at_zy(m, k):
+        return (grp, (z + m + NZ) % NZ * NY + (y + k + NY) % NY)
+
     def partner(e):
         low = grp % NE
         bit0 = (low % 2 + e % 2) % 2
         bit1 = (low // 2 + e // 2) % 2
         return (grp // NE * NE + bit1 * 2 + bit0, seq)
 
-    barrier = pltpu.get_barrier_semaphore()
-    peers = [at_y(k) for k in range(1, NY)]
-    peers += [at_z(m) for m in range(1, NZ)]
-    peers += [partner(e) for e in range(1, NE)]
-    for peer in peers:
-        pl.semaphore_signal(barrier, inc=1, device_id=peer, device_id_type=MESH)
-
     loads = [
         pltpu.make_async_copy(src, dst, load_sem.at[i])
         for i, (src, dst) in enumerate(
@@ -87,6 +86,12 @@
     ]
     for load in loads:
         load.start()
+
+    barrier = pltpu.get_barrier_semaphore()
+    peers = [at_zy(m, k) for m, k in OTHERS]
+    peers += [partner(e) for e in range(1, NE)]
+    for peer in peers:
+        pl.semaphore_signal(barrier, inc=1, device_id=peer, device_id_type=MESH)
 
     started = []
 
@@ -99,10 +104,6 @@
         copy.start()
         started.append(copy)
         return copy
-
-    row, col = iotas((512, 512))
-    p3[...] = onehot(col == row % 32 * 16 + row % 128 // 64 * 8 + row // 128 * 2 + row % 64 // 32)
-    p2[...] = onehot(col == row % 128 // 4 * 16 + row // 128 * 4 + row % 4)
 
     for load in loads[:3]:
         load.wait()
@@ -126,8 +127,10 @@
 
     pl.semaphore_wait(barrier, len(peers))
 
-    fwd_y3 = [send(a3.at[0, 0], a3.at[0, k], Y3 + k - 1, at_y(k)) for k in range(1, NY)]
     fwd_y2 = [send(a2.at[0, :, 0], a2.at[0, :, k], Y2 + k - 1, at_y(k)) for k in range(1, NY)]
+    fwd_s3 = [
+        send(a3.at[0, 0], a3.at[m, k], S3 + m * NY + k, at_zy(m, k)) for m, k in OTHERS
+    ]
     row, col = iotas((32, TOK))
     fwd_y1 = []
     for g in range(GROUPS):
@@ -139,14 +142,23 @@
             [send(a1.at[0, g], a1.at[k, g], Y1 + g * 3 + k - 1, at_y(k)) for k in range(1, NY)]
         )
 
-    for copy in fwd_y3:
-        copy.wait_recv()
-    fwd_z3 = [send(a3.at[0], a3.at[m], Z3 + m - 1, at_z(m)) for m in range(1, NZ)]
+    row, col = iotas((512, 512))
+    p3[...] = onehot(col == row % 32 * 16 + row % 128 // 64 * 8 + row // 128 * 2 + row % 64 // 32)
+    p2[...] = onehot(col == row % 128 // 4 * 16 + row // 128 * 4 + row % 4)
+
     for copy in fwd_y2:
         copy.wait_recv()
     fwd_z2 = []
     for g in range(GROUPS):
         base = Z2 + g * 8
+        if g in DIRECT_F:
+            fwd_z2.append(
+                [
+                    send(a2.at[0, g], a2.at[m, g], base + m, at_z(m))
+                    for m in (4, 3, 5, 2, 6, 1, 7)
+                ]
+            )
+            continue
         fwd_z2.append(
             [
                 send(a2.at[0, g], a2.at[2, g], base, at_z(2)),
@@ -168,8 +180,12 @@
         )
     for load in loads[3:]:
         load.wait()
-
-    for copy in fwd_z3:
+    for h in range(8):
+        cols = slice(h * HD, h * HD + HD)
+        own_s[h] = mm_nt(q_ref[:, cols], k_ref[:, cols])
+        own_d[h] = mm_nt(do_ref[:, cols], v_ref[:, cols])
+
+    for copy in fwd_s3:
         copy.wait_recv()
     t3[0] = mm(p3[...], a3[...].reshape(512, HD)).astype(BF).reshape(GROUPS, TOK, HD)
     fwd_e3 = []
@@ -180,6 +196,8 @@
     half = pl.ds(0, 2)
     rest = pl.ds(2, 2)
     for g in range(GROUPS):
+        if g in DIRECT_F:
+            continue
         base = Z2 + g * 8
         fwd_z2[g][0].wait_recv()
         fwd_z2[g][1].wait_recv()
@@ -190,12 +208,38 @@
             send(a2.at[6, g, rest], a2.at[4, g, rest], base + 7, at_z(-2)),
         ]
 
+    def far_rows(g, hh, kv):
+        part = slice(hh * HD, hh * HD + HD)
+        row2 = (2 * kv + hh) * TOK
+        row3 = kv * 64 + hh * 32
+        return jnp.concatenate(
+            [
+                a1[:, g, kv, :, part].reshape(TOK, HD),
+                kv2[g, row2 : row2 + TOK],
+                t3[:, g, row3 : row3 + 32, :].reshape(TOK, HD),
+            ],
+            axis=0,
+        )
+
+    def finish(g):
+        for hh in range(2):
+            h = 2 * g + hh
+            cols = slice(h * HD, h * HD + HD)
+            weights = kept_w[h]
+            dscores = kept_d[h]
+            keys = jnp.concatenate([k_ref[:, cols], far_rows(g, hh, 0)], axis=0)
+            values = jnp.concatenate([v_ref[:, cols], far_rows(g, hh, 1)], axis=0)
+            o_ref[:, cols] = mm(weights, values).astype(BF)
+            dq_ref[:, cols] = mm(dscores, keys).astype(BF)
+            dk0[:, cols] = mm_tn(dscores[:, :TOK], q_ref[:, cols])
+            dv0[:, cols] = mm_tn(weights[:, :TOK], do_ref[:, cols])
+
     back = FAMILY
     bwd_e3, bwd_z2, bwd_y1 = [], [], []
     for g in range(GROUPS):
         for copy in fwd_y1[g] + fwd_z2[g] + fwd_e3[g]:
             copy.wait_recv()
-        tile2 = mm(p2[...], a2[:, g].reshape(512, HD)).astype(BF)
+        kv2[g] = mm(p2[...], a2[:, g].reshape(512, HD)).astype(BF)
         grads2 = [None] * 4
         for hh in range(2):
             h = 2 * g + hh
@@ -205,44 +249,23 @@
             vrow3 = slice(64 + hh * 32, 64 + hh * 32 + 32)
             q = q_ref[:, cols]
             do = do_ref[:, cols]
-            keys = jnp.concatenate(
-                [
-                    k_ref[:, cols],
-                    a1[:, g, 0, :, part].reshape(TOK, HD),
-                    tile2[hh * TOK : hh * TOK + TOK],
-                    t3[:, g, krow3, :].reshape(TOK, HD),
-                ],
-                axis=0,
-            )
-            values = jnp.concatenate(
-                [
-                    v_ref[:, cols],
-                    a1[:, g, 1, :, part].reshape(TOK, HD),
-                    tile2[256 + hh * TOK : 256 + hh * TOK + TOK],
-                    t3[:, g, vrow3, :].reshape(TOK, HD),
-                ],
-                axis=0,
-            )
-            scores = mm_nt(q, keys) * SCALE
+            scores = jnp.concatenate([own_s[h], mm_nt(q, far_rows(g, hh, 0))], axis=1) * SCALE
+            dshares = jnp.concatenate([own_d[h], mm_nt(do, far_rows(g, hh, 1))], axis=1)
             powers = jnp.exp(scores - jnp.max(scores, axis=1, keepdims=True))
             shares = powers * (1.0 / jnp.sum(powers, axis=1, keepdims=True))
             weights = shares.astype(BF)
-            blended = mm(weights, values)
-            dshares = mm_nt(do, values)
-            deltas = jnp.sum(do.astype(F32) * blended, axis=1, keepdims=True)
+            deltas = jnp.sum(weights.astype(F32) * dshares, axis=1, keepdims=True)
             dscores = (shares * (dshares - deltas) * SCALE).astype(BF)
-            dkeys = mm_tn(dscores, q)
-            dvalues = mm_tn(weights, do)
-            b3s[:, g, krow3, :] = dkeys[3 * TOK :].reshape(NE, 32, HD).astype(BF)
-            b3s[:, g, vrow3, :] = dvalues[3 * TOK :].reshape(NE, 32, HD).astype(BF)
-            b1s[:, g, 0, :, part] = dkeys[TOK : 2 * TOK].reshape(NY, 32, HD).astype(BF)
-            b1s[:, g, 1, :, part] = dvalues[TOK : 2 * TOK].reshape(NY, 32, HD).astype(BF)
-            grads2[hh] = dkeys[2 * TOK : 3 * TOK].astype(BF)
-            grads2[2 + hh] = dvalues[2 * TOK : 3 * TOK].astype(BF)
-            dk0[:, cols] = dkeys[:TOK]
-            dv0[:, cols] = dvalues[:TOK]
-            o_ref[:, cols] = blended.astype(BF)
-            dq_ref[:, cols] = mm(dscores, keys).astype(BF)
+            kept_w[h] = weights
+            kept_d[h] = dscores
+            dkeys = mm_tn(dscores[:, TOK:], q)
+            dvalues = mm_tn(weights[:, TOK:], do)
+            b3s[:, g, krow3, :] = dkeys[2 * TOK :].reshape(NE, 32, HD).astype(BF)
+            b3s[:, g, vrow3, :] = dvalues[2 * TOK :].reshape(NE, 32, HD).astype(BF)
+            b1s[:, g, 0, :, part] = dkeys[:TOK].reshape(NY, 32, HD).astype(BF)
+            b1s[:, g, 1, :, part] = dvalues[:TOK].reshape(NY, 32, HD).astype(BF)
+            grads2[hh] = dkeys[TOK : 2 * TOK].astype(BF)
+            grads2[2 + hh] = dvalues[TOK : 2 * TOK].astype(BF)
         bwd_e3.append(
             [
                 send(b3s.at[e, g], b3r.at[e, g], back + E3 + g * 3 + e - 1, partner(e))
@@ -259,6 +282,14 @@
             mm(p2t[...], jnp.concatenate(grads2, axis=0)).astype(BF).reshape(NZ, NY, 16, HD)
         )
         base = back + Z2 + g * 8
+        if g in DIRECT_B:
+            bwd_z2.append(
+                [
+                    send(b2s.at[m, g], b2r.at[m, g], base + m, at_z(-m))
+                    for m in (4, 3, 5, 2, 6, 1, 7)
+                ]
+            )
+            continue
         bwd_z2.append(
             [
                 send(b2s.at[4, g, half], b2r.at[4, g, half], base, at_z(-2)),
@@ -271,6 +302,8 @@
         )
 
     def relay(g):
+        if g in DIRECT_B:
+            return
         for copy in bwd_z2[g][:4]:
             copy.wait_recv()
         base = back + Z2 + g * 8
@@ -287,6 +320,10 @@
 
     relay(0)
     relay(1)
+    relay(2)
+    finish(0)
+    finish(1)
+    relay(3)
     for copies in bwd_e3:
         for copy in copies:
             copy.wait_recv()
@@ -296,10 +333,21 @@
     c3s[...] = (
         mm(p3t[...], total3.astype(BF).reshape(512, HD)).astype(BF).reshape(NZ, NY, 16, HD)
     )
-    bwd_z3 = [send(c3s.at[m], c3r.at[m], back + Z3 + m - 1, at_z(-m)) for m in range(1, NZ)]
-    relay(2)
-    relay(3)
+    bwd_s3 = [
+        send(c3s.at[m, k], c3r.at[m, k], back + S3 + m * NY + k, at_zy(-m, -k)) for m, k in OTHERS
+    ]
     count = len(started)
+    for g in range(GROUPS):
+        for copy in bwd_z2[g]:
+            copy.wait_recv()
+        total2 = b2s[0, g].astype(F32)
+        for m in range(1, NZ) if g in DIRECT_B else (1, 2, 6, 7):
+            total2 += b2r[m, g].astype(F32)
+        c2s[:, g] = total2.astype(BF)
+    bwd_y2 = [send(c2s.at[k], c2r.at[k], back + Y2 + k - 1, at_y(-k)) for k in range(1, NY)]
+
+    finish(2)
+    finish(3)
     for g in range(GROUPS):
         for copy in bwd_y1[g]:
             copy.wait_recv()
@@ -307,22 +355,6 @@
         for kv, near in enumerate((dk0, dv0)):
             sums1 = jnp.concatenate([b1s[0, g, kv], b1r[1:, g, kv].reshape(96, 256)], axis=0)
             near[:, wide] += mm(place1[g], sums1)
-    for g in range(GROUPS):
-        for copy in bwd_z2[g]:
-            copy.wait_recv()
-        total2 = b2s[0, g].astype(F32)
-        for m in (1, 2, 6, 7):
-            total2 += b2r[m, g].astype(F32)
-        c2s[:, g] = total2.astype(BF)
-    bwd_y2 = [send(c2s.at[k], c2r.at[k], back + Y2 + k - 1, at_y(-k)) for k in range(1, NY)]
-    for copy in bwd_z3:
-        copy.wait_recv()
-    total3 = c3s[0].astype(F32)
-    for m in range(1, NZ):
-        total3 += c3r[m].astype(F32)
-    d3s[...] = total3.astype(BF)
-    bwd_y3 = [send(d3s.at[k], d3r.at[k], back + Y3 + k - 1, at_y(-k)) for k in range(1, NY)]
-
     for copy in started[:count]:
         copy.wait_send()
     for copy in bwd_y2:
@@ -334,11 +366,11 @@
             cols = slice((2 * g + hh) * HD, (2 * g + hh) * HD + HD)
             dk0[:, cols] += spread2[hh * TOK : hh * TOK + TOK]
             dv0[:, cols] += spread2[256 + hh * TOK : 256 + hh * TOK + TOK]
-    for copy in bwd_y3:
+    for copy in bwd_s3:
         copy.wait_recv()
-    sums3 = d3s[0].astype(F32)
-    for k in range(1, NY):
-        sums3 += d3r[k].astype(F32)
+    sums3 = c3s[0, 0].astype(F32)
+    for m, k in OTHERS:
+        sums3 += c3r[m, k].astype(F32)
     row3, _ = iotas((TOK, HD))
     for h in range(8):
         cols = slice(h * HD, h * HD + HD)
@@ -351,20 +383,15 @@
 
 
 def write_out(*refs):
-    sources, targets, held, load_sem, store_sem = refs[:4], refs[4:8], refs[8], refs[9], refs[10]
-    loads = [
-        pltpu.make_async_copy(src, held.at[i], load_sem.at[i]) for i, src in enumerate(sources)
+    sources, targets, sem = refs[:4], refs[4:8], refs[8]
+    copies = [
+        pltpu.make_async_copy(src, dst, sem.at[i])
+        for i, (src, dst) in enumerate(zip(sources, targets))
     ]
-    stores = [
-        pltpu.make_async_copy(held.at[i], dst, store_sem.at[i]) for i, dst in enumerate(targets)
-    ]
-    for load in loads:
-        load.start()
-    for load, store in zip(loads, stores):
-        load.wait()
-        store.start()
-    for store in stores:
-        store.wait()
+    for copy in copies:
+        copy.start()
+    for copy in copies:
+        copy.wait()
 
 
 def on_device(query_vectors, key_vectors, value_vectors, out_grads, offsets):
@@ -374,8 +401,8 @@
     half = lambda *dims: pltpu.VMEM(dims, BF)
     results = pl.pallas_call(
         exchange,
-        out_shape=(shape,) * 4,
-        in_specs=[anywhere] * 5,
+        out_shape=(pltpu.VMEM((TOK, WIDTH), BF),) * 4,
+        in_specs=[pl.BlockSpec(memory_space=pltpu.HBM)] * 5,
         out_specs=(vmem,) * 4,
         scratch_shapes=[
             pltpu.SMEM((3, GROUPS), jnp.int32),
@@ -387,6 +414,9 @@
             half(NZ, GROUPS, NY, 16, HD),
             half(NZ, NY, 16, HD),
             half(NE, GROUPS, TOK, HD),
+            half(GROUPS, 512, HD),
+            half(8, TOK, 4 * TOK),
+            half(8, TOK, 4 * TOK),
             half(NY, GROUPS, 2, 32, 256),
             half(NY, GROUPS, 2, 32, 256),
             half(NZ, GROUPS, NY, 16, HD),
@@ -398,8 +428,8 @@
             half(NE, GROUPS, TOK, HD),
             half(NZ, NY, 16, HD),
             half(NZ, NY, 16, HD),
-            half(NY, 16, HD),
-            half(NY, 16, HD),
+            pltpu.VMEM((8, TOK, TOK), F32),
+            pltpu.VMEM((8, TOK, TOK), F32),
             pltpu.VMEM((TOK, WIDTH), F32),
             pltpu.VMEM((TOK, WIDTH), F32),
             half(512, 512),
@@ -422,14 +452,10 @@
     return pl.pallas_call(
         write_out,
         out_shape=(shape,) * 4,
-        in_specs=[anywhere] * 4,
+        in_specs=[vmem] * 4,
         out_specs=(anywhere,) * 4,
-        scratch_shapes=[
-            half(4, TOK, WIDTH),
-            pltpu.SemaphoreType.DMA((4,)),
-            pltpu.SemaphoreType.DMA((4,)),
-        ],
-        compiler_params=pltpu.CompilerParams(vmem_limit_bytes=60 * 1024 * 1024),
+        scratch_shapes=[pltpu.SemaphoreType.DMA((4,))],
+        compiler_params=pltpu.CompilerParams(vmem_limit_bytes=16 * 1024 * 1024),
         cost_estimate=pl.CostEstimate(
             flops=0, bytes_accessed=2 * 1024 * 1024, transcendentals=0
         ),

time: 56.6 us -> 52.8 us (0.933)
  the two profiles are of different devices: /device:TPU:1 before, /device:TPU:56 now
where the time goes in v3:
time: 52.8 us; the launch traced here: 52.4 us
  Pallas kernels  51.8 us (98%)
  between operations  0.64 us (1%)
    pallas_call x1, Pallas kernels, on_device(): pl.pallas_call(exchange, out_shape=(pltpu.VMEM((TOK, WIDTH), BF),) * 4, i...  50.8 us

profile of v3, /device:TPU:56, one launch (start us, length us, event | category | flops | bytes accessed | tf_op | source)
XLA Modules:
  0.0 52.4 jit_solution(8438173136729163619)
XLA Ops:
  0.6 50.8 %shard_map.84 = (bf16[128,1024]{1,0:T(8,128)(2,1)S(1)}, bf16[128,1024]{1,0:T(8,128)(2,1)S(1)}, bf16[128,1024]{1,0:T(8,128)(2,1)S(1)}, bf16[128,1024]{1,0:T(8,128)(2,1)S(1)}) custom-call(s32[3,4]{1,0:T(4,128)} %off_hbm.1, bf16[128,1024]{1,0:T(8,128)(2,1)} %q_hbm.1, bf16[128,1024]{1,0:T(8,128)(2,1)} %k_hbm.1, bf16[128,1024]{1,0:T(8,128)(2,1)} %v_hbm.1, ...), custom_call_target="tpu_custom_call" | custom-call | flops 1500000000 | bytes 2097152 | tf_op jit(solution)/shard_map/pallas_call | solution.py:402
  51.4 1.0 %shard_map.85 = (bf16[128,1024]{1,0:T(8,128)(2,1)}, bf16[128,1024]{1,0:T(8,128)(2,1)}, bf16[128,1024]{1,0:T(8,128)(2,1)}, bf16[128,1024]{1,0:T(8,128)(2,1)}) custom-call(bf16[128,1024]{1,0:T(8,128)(2,1)S(1)} %get-tuple-element.8.refs_0_, bf16[128,1024]{1,0:T(8,128)(2,1)S(1)} %get-tuple-element.9.refs_1_, bf16[128,1024]{1,0:T(8,128)(2,1)S(1)} %get-tuple-element.10.refs_2_, ...), custom_call_target="tpu_custom_call" | custom-call | bytes 2097152 | tf_op jit(solution)/shard_map/pallas_call | solution.py:452

commit v4 on v3

--- a/solution.py
+++ b/solution.py
@@ -21,8 +21,6 @@
 
 S3, Y2, Y1, Z2, E3 = 0, 32, 35, 47, 79
 FAMILY = 91
-DIRECT_F = (0, 1, 2, 3)
-DIRECT_B = ()
 OTHERS = [(m, k) for m in (4, 3, 5, 2, 6, 1, 7, 0) for k in (3, 2, 1, 0) if (m, k) != (0, 0)]
 
 
@@ -78,21 +76,21 @@
         bit1 = (low // 2 + e // 2) % 2
         return (grp // NE * NE + bit1 * 2 + bit0, seq)
 
-    loads = [
-        pltpu.make_async_copy(src, dst, load_sem.at[i])
-        for i, (src, dst) in enumerate(
-            ((off_hbm, off), (k_hbm, k_ref), (v_hbm, v_ref), (q_hbm, q_ref), (do_hbm, do_ref))
-        )
-    ]
-    for load in loads:
-        load.start()
-
     barrier = pltpu.get_barrier_semaphore()
     peers = [at_zy(m, k) for m, k in OTHERS]
     peers += [partner(e) for e in range(1, NE)]
     for peer in peers:
         pl.semaphore_signal(barrier, inc=1, device_id=peer, device_id_type=MESH)
 
+    loads = [
+        pltpu.make_async_copy(src, dst, load_sem.at[i])
+        for i, (src, dst) in enumerate(
+            ((off_hbm, off), (k_hbm, k_ref), (v_hbm, v_ref), (q_hbm, q_ref), (do_hbm, do_ref))
+        )
+    ]
+    for load in loads:
+        load.start()
+
     started = []
 
     def send(src, dst, index, device):
@@ -105,6 +103,8 @@
         started.append(copy)
         return copy
 
+    row, col = iotas((512, 512))
+    p3[...] = onehot(col == row % 32 * 16 + row % 128 // 64 * 8 + row // 128 * 2 + row % 64 // 32)
     for load in loads[:3]:
         load.wait()
     row, col = iotas((32, TOK))
@@ -142,48 +142,14 @@
             [send(a1.at[0, g], a1.at[k, g], Y1 + g * 3 + k - 1, at_y(k)) for k in range(1, NY)]
         )
 
-    row, col = iotas((512, 512))
-    p3[...] = onehot(col == row % 32 * 16 + row % 128 // 64 * 8 + row // 128 * 2 + row % 64 // 32)
-    p2[...] = onehot(col == row % 128 // 4 * 16 + row // 128 * 4 + row % 4)
-
     for copy in fwd_y2:
         copy.wait_recv()
     fwd_z2 = []
     for g in range(GROUPS):
         base = Z2 + g * 8
-        if g in DIRECT_F:
-            fwd_z2.append(
-                [
-                    send(a2.at[0, g], a2.at[m, g], base + m, at_z(m))
-                    for m in (4, 3, 5, 2, 6, 1, 7)
-                ]
-            )
-            continue
         fwd_z2.append(
-            [
-                send(a2.at[0, g], a2.at[2, g], base, at_z(2)),
-                send(a2.at[0, g], a2.at[6, g], base + 1, at_z(-2)),
-                send(a2.at[0, g], a2.at[1, g], base + 2, at_z(1)),
-                send(a2.at[0, g], a2.at[7, g], base + 3, at_z(-1)),
-            ]
-        )
-
-    row, col = iotas((512, 512))
-    p3t[...] = onehot(row == col % 32 * 16 + col % 128 // 64 * 8 + col // 128 * 2 + col % 64 // 32)
-    p2t[...] = onehot(row == col % 128 // 4 * 16 + col // 128 * 4 + col % 4)
-    row1, col1 = iotas((TOK, TOK))
-    row2, col2 = iotas((512, NY * 16))
-    for g in range(GROUPS):
-        place1[g] = onehot(row1 == 4 * (col1 % 32) + off[0, g])
-        place2[g] = onehot(
-            (col2 % 16 // 4 == row2 // 128) & (row2 % 128 == 32 * (col2 % 4) + off[1, g])
-        )
-    for load in loads[3:]:
-        load.wait()
-    for h in range(8):
-        cols = slice(h * HD, h * HD + HD)
-        own_s[h] = mm_nt(q_ref[:, cols], k_ref[:, cols])
-        own_d[h] = mm_nt(do_ref[:, cols], v_ref[:, cols])
+            [send(a2.at[0, g], a2.at[m, g], base + m, at_z(m)) for m in (4, 3, 5, 2, 6, 1, 7)]
+        )
 
     for copy in fwd_s3:
         copy.wait_recv()
@@ -191,23 +157,8 @@
     fwd_e3 = []
     for g in range(GROUPS):
         fwd_e3.append(
-            [send(t3.at[0, g], t3.at[e, g], E3 + g * 3 + e - 1, partner(e)) for e in range(1, NE)]
-        )
-    half = pl.ds(0, 2)
-    rest = pl.ds(2, 2)
-    for g in range(GROUPS):
-        if g in DIRECT_F:
-            continue
-        base = Z2 + g * 8
-        fwd_z2[g][0].wait_recv()
-        fwd_z2[g][1].wait_recv()
-        fwd_z2[g] = fwd_z2[g][2:] + [
-            send(a2.at[2, g], a2.at[3, g], base + 4, at_z(1)),
-            send(a2.at[6, g], a2.at[5, g], base + 5, at_z(-1)),
-            send(a2.at[2, g, half], a2.at[4, g, half], base + 6, at_z(2)),
-            send(a2.at[6, g, rest], a2.at[4, g, rest], base + 7, at_z(-2)),
-        ]
-
+            [send(t3.at[0, g], t3.at[e, g], E3 + g * 3 + e - 1, partner(e)) for e in (2, 3, 1)]
+        )
     def far_rows(g, hh, kv):
         part = slice(hh * HD, hh * HD + HD)
         row2 = (2 * kv + hh) * TOK
@@ -234,7 +185,20 @@
             dk0[:, cols] = mm_tn(dscores[:, :TOK], q_ref[:, cols])
             dv0[:, cols] = mm_tn(weights[:, :TOK], do_ref[:, cols])
 
+    row, col = iotas((512, 512))
+    p2[...] = onehot(col == row % 128 // 4 * 16 + row // 128 * 4 + row % 4)
+
+    p2t[...] = onehot(row == col % 128 // 4 * 16 + col // 128 * 4 + col % 4)
+    for load in loads[3:]:
+        load.wait()
+    for h in range(8):
+        cols = slice(h * HD, h * HD + HD)
+        own_s[h] = mm_nt(q_ref[:, cols], k_ref[:, cols])
+        own_d[h] = mm_nt(do_ref[:, cols], v_ref[:, cols])
+
     back = FAMILY
+    half = pl.ds(0, 2)
+    rest = pl.ds(2, 2)
     bwd_e3, bwd_z2, bwd_y1 = [], [], []
     for g in range(GROUPS):
         for copy in fwd_y1[g] + fwd_z2[g] + fwd_e3[g]:
@@ -266,30 +230,22 @@
             b1s[:, g, 1, :, part] = dvalues[:TOK].reshape(NY, 32, HD).astype(BF)
             grads2[hh] = dkeys[TOK : 2 * TOK].astype(BF)
             grads2[2 + hh] = dvalues[TOK : 2 * TOK].astype(BF)
-        bwd_e3.append(
-            [
-                send(b3s.at[e, g], b3r.at[e, g], back + E3 + g * 3 + e - 1, partner(e))
-                for e in range(1, NE)
-            ]
-        )
         bwd_y1.append(
             [
                 send(b1s.at[k, g], b1r.at[k, g], back + Y1 + g * 3 + k - 1, at_y(-k))
                 for k in range(1, NY)
             ]
         )
+        bwd_e3.append(
+            [
+                send(b3s.at[e, g], b3r.at[e, g], back + E3 + g * 3 + e - 1, partner(e))
+                for e in (2, 3, 1)
+            ]
+        )
         b2s[:, g] = (
             mm(p2t[...], jnp.concatenate(grads2, axis=0)).astype(BF).reshape(NZ, NY, 16, HD)
         )
         base = back + Z2 + g * 8
-        if g in DIRECT_B:
-            bwd_z2.append(
-                [
-                    send(b2s.at[m, g], b2r.at[m, g], base + m, at_z(-m))
-                    for m in (4, 3, 5, 2, 6, 1, 7)
-                ]
-            )
-            continue
         bwd_z2.append(
             [
                 send(b2s.at[4, g, half], b2r.at[4, g, half], base, at_z(-2)),
@@ -302,8 +258,6 @@
         )
 
     def relay(g):
-        if g in DIRECT_B:
-            return
         for copy in bwd_z2[g][:4]:
             copy.wait_recv()
         base = back + Z2 + g * 8
@@ -320,6 +274,8 @@
 
     relay(0)
     relay(1)
+    row, col = iotas((512, 512))
+    p3t[...] = onehot(row == col % 32 * 16 + col % 128 // 64 * 8 + col // 128 * 2 + col % 64 // 32)
     relay(2)
     finish(0)
     finish(1)
@@ -341,13 +297,20 @@
         for copy in bwd_z2[g]:
             copy.wait_recv()
         total2 = b2s[0, g].astype(F32)
-        for m in range(1, NZ) if g in DIRECT_B else (1, 2, 6, 7):
+        for m in (1, 2, 6, 7):
             total2 += b2r[m, g].astype(F32)
         c2s[:, g] = total2.astype(BF)
     bwd_y2 = [send(c2s.at[k], c2r.at[k], back + Y2 + k - 1, at_y(-k)) for k in range(1, NY)]
 
     finish(2)
     finish(3)
+    row1, col1 = iotas((TOK, TOK))
+    row2, col2 = iotas((512, NY * 16))
+    for g in range(GROUPS):
+        place1[g] = onehot(row1 == 4 * (col1 % 32) + off[0, g])
+        place2[g] = onehot(
+            (col2 % 16 // 4 == row2 // 128) & (row2 % 128 == 32 * (col2 % 4) + off[1, g])
+        )
     for g in range(GROUPS):
         for copy in bwd_y1[g]:
             copy.wait_recv()

time: 52.8 us -> 52.6 us (level)
  no operation moved by 1% of the time
where the time goes in v4:
time: 52.6 us; the launch traced here: 52.5 us
  Pallas kernels  51.8 us (98%)
  between operations  0.64 us (1%)
    pallas_call x1, Pallas kernels, on_device(): pl.pallas_call(exchange, out_shape=(pltpu.VMEM((TOK, WIDTH), BF),) * 4, i...  50.8 us

profile of v4, /device:TPU:56, one launch (start us, length us, event | category | flops | bytes accessed | tf_op | source)
XLA Modules:
  0.0 52.5 jit_solution(7273772285681467008)
XLA Ops:
  0.6 50.8 %shard_map.84 = (bf16[128,1024]{1,0:T(8,128)(2,1)S(1)}, bf16[128,1024]{1,0:T(8,128)(2,1)S(1)}, bf16[128,1024]{1,0:T(8,128)(2,1)S(1)}, bf16[128,1024]{1,0:T(8,128)(2,1)S(1)}) custom-call(s32[3,4]{1,0:T(4,128)} %off_hbm.1, bf16[128,1024]{1,0:T(8,128)(2,1)} %q_hbm.1, bf16[128,1024]{1,0:T(8,128)(2,1)} %k_hbm.1, bf16[128,1024]{1,0:T(8,128)(2,1)} %v_hbm.1, ...), custom_call_target="tpu_custom_call" | custom-call | flops 1500000000 | bytes 2097152 | tf_op jit(solution)/shard_map/pallas_call | solution.py:365
  51.5 1.0 %shard_map.85 = (bf16[128,1024]{1,0:T(8,128)(2,1)}, bf16[128,1024]{1,0:T(8,128)(2,1)}, bf16[128,1024]{1,0:T(8,128)(2,1)}, bf16[128,1024]{1,0:T(8,128)(2,1)}) custom-call(bf16[128,1024]{1,0:T(8,128)(2,1)S(1)} %get-tuple-element.8.refs_0_, bf16[128,1024]{1,0:T(8,128)(2,1)S(1)} %get-tuple-element.9.refs_1_, bf16[128,1024]{1,0:T(8,128)(2,1)S(1)} %get-tuple-element.10.refs_2_, ...), custom_call_target="tpu_custom_call" | custom-call | bytes 2097152 | tf_op jit(solution)/shard_map/pallas_call | solution.py:415
